TPU v7x, 256 devices: a whole 4x4x8 slice. The times are simulated.
256 devices in a mesh: rep: 4 (over z_hi), fsdp: 64 (over y, z_lo, x, core).
Axes of the slice: x: 4, y: 4, z: 8 (z_hi: 4, z_lo: 2; z = z_hi * 2 + z_lo), core: 2. Of those that a mesh axis runs over, the one named last changes fastest.
Arguments:
- tokens: bfloat16 [4, 16384, 9216], P('rep', 'fsdp'), may hold values from -16 to 16
- norm_gain: float32 [9216], replicated, may hold values from 0.1 to 1.9
- master_weight: float32 [4, 9216, 512], P('rep', 'fsdp'), may hold values from -0.0625 to 0.0625
- inner_moment: float32 [4, 9216, 512], P('rep', 'fsdp'), may hold values from -4 to 4
- inner_second: float32 [4, 9216, 512], P('rep', 'fsdp'), may hold values from 0.1 to 1
- cotangent: bfloat16 [4, 16384, 512], P('rep', 'fsdp'), may hold values from -0.125 to 0.125
- frag_global: float32 [2, 9216, 512], P(None, 'fsdp'), may hold values from -6 to 6
- frag_local: float32 [4, 2, 9216, 512], P('rep', None, 'fsdp'), may hold values from -6 to 6
- outer_momentum: float32 [2, 9216, 512], P(None, 'fsdp'), may hold values from -6 to 6
- fragment_index: int32 [1], replicated, may hold values from 0 to 511
Outputs:
- key_out: bfloat16 [4, 16384, 512], P('rep', 'fsdp')
- new_master: float32 [4, 9216, 512], P('rep', 'fsdp')
- new_moment: float32 [4, 9216, 512], P('rep', 'fsdp')
- new_second: float32 [4, 9216, 512], P('rep', 'fsdp')
- new_global: float32 [9216, 512], P('fsdp')
- new_outer: float32 [9216, 512], P('fsdp')
All inputs are finite; a program needn't handle non-finite values.
Results may differ from a plain program's by a relative error of at most 0.0065.
Values may be sent and summed in bfloat16 or wider, within the bound.
A program may use at most 128 MiB of HBM per device.

v0:
```python
import jax
import jax.numpy as jnp
from jax import lax
from jax.sharding import PartitionSpec as P


def shards(
    tokens,
    norm_gain,
    master_weight,
    inner_moment,
    inner_second,
    cotangent,
    frag_global,
    frag_local,
    outer_momentum,
    fragment_index,
):
    values = tokens[0].astype(jnp.float32)
    inverse_rms = lax.rsqrt(jnp.mean(values * values, axis=-1, keepdims=True) + 1e-05)
    normed = (values * inverse_rms * norm_gain).astype(jnp.bfloat16)
    master = master_weight[0]
    weight_bf = master.astype(jnp.bfloat16)
    feature_cols = normed
    key_rows = jnp.dot(
        feature_cols,
        lax.all_gather(weight_bf, "fsdp", axis=0, tiled=True),
        preferred_element_type=jnp.float32,
    )
    upstream = cotangent[0]
    feature_cols = normed
    grad = lax.psum_scatter(
        lax.dot_general(
            feature_cols, upstream, (((0,), (0,)), ((), ())), preferred_element_type=jnp.float32
        ),
        "fsdp",
        scatter_dimension=0,
        tiled=True,
    )
    moment_next = 0.9 * inner_moment[0] + 0.1 * grad
    second_next = 0.95 * inner_second[0] + 0.05 * grad * grad
    master_next = master - 0.02 * (moment_next / (jnp.sqrt(second_next) + 1e-08) + 0.1 * master)
    frag_total = frag_global.shape[0]
    outer_step = fragment_index[0]
    frag_pick = outer_step % frag_total
    round_count = (outer_step // frag_total).astype(jnp.float32)
    outer_rate = 0.7 * (1.0 - round_count / 512.0)
    frag_now = lax.dynamic_index_in_dim(frag_global, frag_pick, 0, keepdims=False)
    local_now = lax.dynamic_index_in_dim(frag_local[0], frag_pick, 0, keepdims=False)
    moment_now = lax.dynamic_index_in_dim(outer_momentum, frag_pick, 0, keepdims=False)
    pseudo_local = frag_now - local_now
    replicas = lax.axis_size("rep")
    pseudo_grad = lax.psum(pseudo_local, "rep") / replicas
    new_outer = 0.9 * moment_now + pseudo_grad
    new_global = frag_now - outer_rate * (pseudo_grad + 0.9 * new_outer)
    return (
        key_rows.astype(jnp.bfloat16)[None],
        master_next[None],
        moment_next[None],
        second_next[None],
        new_global,
        new_outer,
    )


def solution(mesh):
    in_specs = (
        P("rep", "fsdp", None),
        P(),
        P("rep", "fsdp", None),
        P("rep", "fsdp", None),
        P("rep", "fsdp", None),
        P("rep", "fsdp", None),
        P(None, "fsdp", None),
        P("rep", None, "fsdp", None),
        P(None, "fsdp", None),
        P(),
    )
    out_specs = (
        P("rep", "fsdp", None),
        P("rep", "fsdp", None),
        P("rep", "fsdp", None),
        P("rep", "fsdp", None),
        P("fsdp", None),
        P("fsdp", None),
    )
    return jax.shard_map(shards, mesh=mesh, in_specs=in_specs, out_specs=out_specs, check_vma=False)
```

profile of v0, /device:TPU:1, one launch (start us, length us, event | category | flops | bytes accessed | tf_op | source)
XLA Modules:
  0.0 456.0 jit_solution(5907639696820063332)
XLA Ops:
  8.0 0.0 copy-start
  8.0 0.0 all-reduce.2.cloned.1.call-start
  8.8 1.8 bitcast_subtract_fusion
  10.6 0.0 all-reduce.2.cloned.1.call-update
  10.6 0.0 all-gather.2.cloned.1.call-start
  10.6 1.6 bitcast_convert_fusion
  12.3 0.0 all-gather.2.cloned.1.call-update
  12.3 0.0 reduce-scatter.2.cloned.1.call-start
  12.4 3.4 fusion.2
  15.7 0.0 copy-done
  15.7 10.5 %fusion.8 = f32[9216,512]{1,0:T(8,128)} fusion(bf16[1,256,9216]{2,1,0:T(8,128)(2,1)} %param.10, f32[9216]{0:T(1024)} %param.11, f32[256]{0:T(256)S(1)} %add_rsqrt_fusion, bf16[1,256,512]{2,1,0:T(8,128)(2,1)S(1)} %copy-done), kind=kOutput, calls=%fused_computation.10 | convolution fusion | flops 2425356288 | bytes 23892992 | tf_op jit(solution)/shard_map/dot_general | solution.py:33
  26.3 0.0 copy-start.2
  26.3 0.0 copy-start.5
  26.3 0.0 copy-start.6
  26.3 0.0 reduce-scatter.2.cloned.1.call-update
  26.3 40.0 %all-reduce.2.cloned.1.call-done = f32[144,512]{1,0:T(8,128)} async-done(((f32[144,512]{1,0:T(8,128)}), f32[144,512]{1,0:T(8,128)}) %all-reduce.2.cloned.1.call-update) | async-done | bytes 294928 | tf_op jit(solution)/shard_map/psum | solution.py:53
  66.3 0.0 copy-done.2
  66.3 0.0 copy-done.5
  66.3 1.9 bitcast_subtract_fusion.1
  68.2 0.0 copy-start.1
  68.2 0.0 copy-start.3
  68.2 0.0 copy-start.4
  68.2 65.8 %all-gather.2.cloned.1.call-done = bf16[9216,512]{1,0:T(8,128)(2,1)} async-done(((bf16[144,512]{1,0:T(8,128)(2,1)}), bf16[9216,512]{1,0:T(8,128)(2,1)}) %all-gather.2.cloned.1.call-update) | async-done | bytes 9437200 | tf_op jit(solution)/shard_map/all_gather | solution.py:27
  134.0 0.0 copy-done.6
  134.0 8.5 %fusion.19 = bf16[1,256,512]{2,1,0:T(8,128)(2,1)} fusion(bf16[9216,512]{1,0:T(8,128)(2,1)} %all-gather.2.cloned.1.call-done, bf16[1,256,9216]{2,1,0:T(8,128)(2,1)} %param.10, f32[9216]{0:T(1024)S(1)} %copy-done.6, f32[256]{0:T(256)S(1)} %add_rsqrt_fusion), kind=kOutput, calls=%fused_computation.17 | convolution fusion | flops 2425487360 | bytes 14455808 | tf_op jit(solution)/shard_map/dot_general | solution.py:25
  142.5 304.0 %reduce-scatter.2.cloned.1.call-done = f32[144,512]{1,0:T(8,128)} async-done(((f32[9216,512]{1,0:T(8,128)}), f32[144,512]{1,0:T(8,128)}) %reduce-scatter.2.cloned.1.call-update) | async-done | bytes 294928 | tf_op jit(solution)/shard_map/reduce_scatter | solution.py:32
  446.5 0.0 copy-done.1
  446.5 0.0 copy-done.3
  446.5 0.0 copy-done.4
  446.5 2.1 fusion.28
  (1 shorter events, 0.0 us)
Async XLA Ops:
  8.0 7.7 %copy-start = (bf16[1,256,512]{2,1,0:T(8,128)(2,1)S(1)}, bf16[1,256,512]{2,1,0:T(8,128)(2,1)}, u32[]{:S(2)}) copy-start(bf16[1,256,512]{2,1,0:T(8,128)(2,1)} %param.15) | copy-start | bytes 786436
  8.0 58.3 %all-reduce.2.cloned.1.call-start = ((), (), s32[]{:S(2)}) async-start(), calls=%async_computation.3 | async-start | bytes 589824 | tf_op jit(solution)/shard_map/psum | solution.py:53
  10.6 123.4 %all-gather.2.cloned.1.call-start = ((), (), s32[]{:S(2)}) async-start(), calls=%async_computation.1 | async-start | bytes 9584640 | tf_op jit(solution)/shard_map/all_gather | solution.py:27
  12.3 434.1 %reduce-scatter.2.cloned.1.call-start = ((), (), s32[]{:S(2)}) async-start(), calls=%async_computation.2 | async-start | bytes 19169280 | tf_op jit(solution)/shard_map/reduce_scatter | solution.py:32
  26.3 40.1 %copy-start.2 = (f32[2,144,512]{2,1,0:T(8,128)S(1)}, f32[2,144,512]{2,1,0:T(8,128)}, u32[]{:S(2)}) copy-start(f32[2,144,512]{2,1,0:T(8,128)} %param.16) | copy-start | bytes 1769476
  26.3 40.1 %copy-start.5 = (f32[2,144,512]{2,1,0:T(8,128)S(1)}, f32[2,144,512]{2,1,0:T(8,128)}, u32[]{:S(2)}) copy-start(f32[2,144,512]{2,1,0:T(8,128)} %param.18) | copy-start | bytes 1769476
  26.3 107.7 %copy-start.6 = (f32[9216]{0:T(1024)S(1)}, f32[9216]{0:T(1024)}, u32[]{:S(2)}) copy-start(f32[9216]{0:T(1024)} %param.11) | copy-start | bytes 110596
  68.2 378.3 %copy-start.1 = (f32[1,144,512]{2,1,0:T(8,128)S(1)}, f32[1,144,512]{2,1,0:T(8,128)}, u32[]{:S(2)}) copy-start(f32[1,144,512]{2,1,0:T(8,128)} %param.12) | copy-start | bytes 884740
  68.2 378.3 %copy-start.3 = (f32[1,144,512]{2,1,0:T(8,128)S(1)}, f32[1,144,512]{2,1,0:T(8,128)}, u32[]{:S(2)}) copy-start(f32[1,144,512]{2,1,0:T(8,128)} %param.14) | copy-start | bytes 884740
  68.2 378.3 %copy-start.4 = (f32[1,144,512]{2,1,0:T(8,128)S(1)}, f32[1,144,512]{2,1,0:T(8,128)}, u32[]{:S(2)}) copy-start(f32[1,144,512]{2,1,0:T(8,128)} %param.13) | copy-start | bytes 884740
Sparse Core Ops, SparseCore 0:
  12.1 54.2 all-reduce.1
Sparse Core Ops, SparseCore 1:
  13.5 120.4 all-gather.1
  136.4 310.0 reduce-scatter.1
where the time goes:
time: 461 us; the launch traced here: 456 us
  waiting for transfers between devices  410 us (89%)
  matrix products  19 us (4%)
  between operations  16.2 us (4%)
  other arithmetic  10.8 us (2%)
    reduce_scatter x1, waiting for transfers between devices, shards(): lax.psum_scatter(lax.dot_general(feature_cols, upstream, (((0,), (0,)), (...  304 us
    all_gather x1, waiting for transfers between devices, shards(): lax.all_gather(weight_bf, 'fsdp', axis=0, tiled=True)  65.8 us
    psum x1, waiting for transfers between devices, shards(): pseudo_grad = lax.psum(pseudo_local, 'rep') / replicas  40 us
    dot_general x1, matrix products, shards(): lax.dot_general(feature_cols, upstream, (((0,), (0,)), ((), ())), preferr...  10.5 us
  transfers between devices with their start and end apart: 3, of which 3 were waited for; matrix products, arithmetic and copies ran while one was open for 6% of the time, Pallas kernels for 0%

commit v1 on v0

v1 whole, which is shorter than its diff:
```python
import functools

import jax
import jax.numpy as jnp
from jax import lax
from jax.experimental import pallas as pl
from jax.experimental.pallas import tpu as pltpu
from jax.sharding import PartitionSpec as P

MESH = pl.DeviceIdType.MESH
F32 = jnp.float32
BF16 = jnp.bfloat16
REPS = 4
SIDE = 4
PLANES = 2
STRIP = 32
N_SEMS = 160


def kernel(
    tokens_hbm, gain_hbm, master_hbm, cot_hbm, global_hbm, local_hbm, index_ref,
    key_ref, grad_ref, pseudo_ref,
    tok, gain, master, frag_now, frag_local, cot, cot_oth,
    w_own, w, norm, norm_oth, part, part_bf, e_in, s_in, s_sum, s_bf, e2_in, s2_in,
    t_sum, t_bf, z_in, key_own, key_oth, key_in, diffs,
    in_sem, send_sem, recv_sem,
):
    rows, cols = master.shape
    n_tok = tok.shape[0]
    half = cols // 2
    lo, hi = pl.ds(0, half), pl.ds(half, half)
    group = norm.shape[-1]
    pair = PLANES * rows

    me = lax.axis_index("fsdp")
    rep = lax.axis_index("rep")
    core = me % 2
    x = (me // 2) % SIDE
    z = (me // (2 * SIDE)) % PLANES
    y = me // (2 * SIDE * PLANES)
    home = core == z

    def dev(y_, z_, x_, c_):
        return {"fsdp": ((y_ * PLANES + z_) * SIDE + x_) * 2 + c_}

    def along(axis, step):
        if axis == "x":
            return dev(y, z, (x + step + SIDE) % SIDE, core)
        return dev((y + step + SIDE) % SIDE, z, x, core)

    count = [0]
    started = []

    def slot():
        count[0] += 1
        return count[0] - 1

    def push(src, dst, to, sem=None, recv=None):
        sem = slot() if sem is None else sem
        copy = pltpu.make_async_remote_copy(
            src_ref=src,
            dst_ref=dst,
            send_sem=send_sem.at[sem],
            recv_sem=recv_sem.at[sem if recv is None else recv],
            device_id=to,
            device_id_type=MESH,
        )
        copy.start()
        return copy

    def send(src, dst, to):
        copy = push(src, dst, to)
        started.append(copy)
        return copy

    loads = []

    def load(src, dst):
        copy = pltpu.make_async_copy(src, dst, in_sem.at[len(loads)])
        copy.start()
        loads.append(copy)
        return copy

    load_master = load(master_hbm, master)
    n_chunk = 4
    chunk = n_tok // n_chunk
    load_gain = load(gain_hbm, gain)
    load_tok = [load(tokens_hbm.at[pl.ds(i * chunk, chunk)], tok.at[pl.ds(i * chunk, chunk)]) for i in range(n_chunk)]
    load_cot = load(cot_hbm, cot)
    load_now = load(global_hbm, frag_now)
    load_loc = load(local_hbm, frag_local)

    barrier = pltpu.get_barrier_semaphore()
    other_core = dev(y, z, x, 1 - core)
    peers = [along("x", 1), along("x", -1), along("y", 1), along("y", -1), other_core,
             dev(y, 1 - z, x, core), dev(y, 1 - z, x, 1 - core)]
    peers += [{"rep": (rep + k) % REPS} for k in range(1, REPS)]
    for peer in peers:
        pl.semaphore_signal(barrier, inc=1, device_id=peer, device_id_type=MESH)

    load_master.wait()
    w_own[...] = master[...].astype(BF16)
    pl.semaphore_wait(barrier, len(peers))

    def w_rows(y_, x_, c_):
        return y_, pl.ds(pl.multiple_of(x_ * pair + c_ * rows, 16), rows)

    own_at = w.at[w_rows(y, x, core)]
    w_far, w_near = slot(), slot()
    w_got = (slot(), slot())
    far_copy = push(w_own, own_at, dev(y, 1 - z, x, z), w_far, w_got[0] + core)

    @pl.when(home)
    def _():
        w[w_rows(y, x, core)] = w_own[...]

    @pl.when(jnp.logical_not(home))
    def _():
        push(w_own, own_at, other_core, w_near, w_got[0] + core)

    load_cot.wait()
    cot_copy = send(cot, cot_oth, other_core)

    tiles = group // 128
    n_group = norm.shape[0] * norm.shape[1]
    width = n_group * group

    def normalise(i):
        load_tok[i].wait()

        @pl.loop(0, chunk // STRIP)
        def _(s):
            at = pl.ds(pl.multiple_of(i * chunk + s * STRIP, STRIP), STRIP)
            total = jnp.zeros((STRIP, 128), F32)
            for t in range(width // 128):
                v = tok[at, t * 128:(t + 1) * 128].astype(F32)
                total = total + v * v
            mean = jnp.sum(total, axis=-1, keepdims=True) / width
            inverse = lax.rsqrt(mean + 1e-05)
            for t in range(width // 128):
                g, l = t // tiles, t % tiles
                v = tok[at, t * 128:(t + 1) * 128].astype(F32)
                v = v * inverse * gain[:, t * 128:(t + 1) * 128]
                norm[g // PLANES, g % PLANES, at, l * 128:(l + 1) * 128] = v.astype(BF16)

    load_gain.wait()
    normalise(0)

    first, second = ("x", "y"), ("y", "x")
    at1, at2 = (x, y), (y, x)

    def block(hf, a, b):
        y_, x_ = (b, a) if hf == 0 else (a, b)
        return w_rows(y_ % SIDE, x_ % SIDE, hf)

    def cut(where, columns):
        return (*where, columns)

    STEP = (1, -1)
    SIDE_COLS = (lo, hi)
    for c_ in range(2):
        @pl.when(jnp.logical_not(jnp.logical_and(home, core == c_)))
        def _():
            pltpu.make_async_remote_copy(
                src_ref=w_own, dst_ref=own_at, send_sem=send_sem.at[w_far], recv_sem=recv_sem.at[w_got[c_]],
                device_id=other_core, device_id_type=MESH).wait_recv()

    def gather_second(hf, a):
        ref = w.at[block(hf, a, at2[hf])]
        return [send(ref, ref, along(second[hf], STEP[d])) for d in range(2)]

    def gather_forward(hf, copies, a):
        out = []
        for d in range(2):
            copies[d].wait_recv()
            ref = w.at[cut(block(hf, a, at2[hf] - STEP[d] + SIDE), SIDE_COLS[d])]
            out.append(send(ref, ref, along(second[hf], STEP[d])))
        return out

    one = []
    for hf in range(2):
        ref = w.at[block(hf, at1[hf], at2[hf])]
        one.append([send(ref, ref, along(first[hf], STEP[d])) for d in range(2)])
    two = [[gather_second(hf, at1[hf])] for hf in range(2)]

    for i in range(1, n_chunk):
        normalise(i)
    norm_copies = [send(norm.at[q, 1 - core], norm_oth.at[q], other_core) for q in range(SIDE)]

    load_now.wait()
    load_loc.wait()
    k = index_ref[0] % frag_now.shape[0]
    diffs[rep] = (frag_now[k] - frag_local[k]).astype(BF16)
    rep_copies = [send(diffs.at[rep], diffs.at[rep], {"rep": (rep + j) % REPS}) for j in range(1, REPS)]

    one_f = [[None, None], [None, None]]
    for hf in range(2):
        for d in range(2):
            one[hf][d].wait_recv()
            a = at1[hf] - STEP[d] + SIDE
            ref = w.at[cut(block(hf, a, at2[hf]), SIDE_COLS[d])]
            one_f[hf][d] = send(ref, ref, along(first[hf], STEP[d]))
            two[hf].append(gather_second(hf, a))

    piece = group // 3
    over_tokens = (((0,), (0,)), ((), ()))

    @pl.loop(0, SIDE)
    def _(q):
        for j in range(3):
            part[q, j * piece:(j + 1) * piece, :] = lax.dot_general(
                norm[q, core, :, j * piece:(j + 1) * piece], cot[...], over_tokens, preferred_element_type=F32)

    two_f = [[None] * SIDE, [None] * SIDE]
    for hf in range(2):
        two_f[hf][0] = gather_forward(hf, two[hf][0], at1[hf])
    for hf in range(2):
        for d in range(2):
            one_f[hf][d].wait_recv()
        two[hf].append(gather_second(hf, at1[hf] + 2))

    cot_copy.wait_recv()
    for copy in norm_copies:
        copy.wait_recv()

    @pl.loop(0, SIDE)
    def _(q):
        for j in range(3):
            total = part[q, j * piece:(j + 1) * piece, :] + lax.dot_general(
                norm_oth[q, :, j * piece:(j + 1) * piece], cot_oth[...], over_tokens, preferred_element_type=F32)
            part[q, j * piece:(j + 1) * piece, :] = total
            part_bf[q, j * piece:(j + 1) * piece, :] = total.astype(BF16)

    rel = (0, -1, 1, 2)
    for hf in range(2):
        for i in range(1, SIDE):
            two_f[hf][i] = gather_forward(hf, two[hf][i], at1[hf] + rel[i] + SIDE)

    order = (3, 2, 1, 0)
    e_copies = [[None] * SIDE, [None] * SIDE]
    d_copies = [[None] * SIDE, [None] * SIDE]
    for i in order:
        for hf in range(2):
            a = at1[hf] + rel[i] + SIDE
            e_copies[hf][i] = [
                send(part_bf.at[cut(block(hf, a, at2[hf] + 2), SIDE_COLS[d])], e_in.at[hf, d, i], along(second[hf], STEP[d]))
                for d in range(2)]
    for i in order:
        for hf in range(2):
            a = at1[hf] + rel[i] + SIDE
            d_copies[hf][i] = [
                send(part_bf.at[cut(block(hf, a, at2[hf] + STEP[d] + SIDE), SIDE_COLS[1 - d])],
                     s_in.at[hf, d, i, :, SIDE_COLS[1 - d]], along(second[hf], STEP[d]))
                for d in range(2)]

    for hf in range(2):
        for i in range(SIDE):
            for copy in two_f[hf][i]:
                copy.wait_recv()

    def keys(operand):
        total = jnp.dot(operand(0), w[0], preferred_element_type=F32)
        for q in range(1, SIDE):
            total = total + jnp.dot(operand(q), w[q], preferred_element_type=F32)
        return total

    key_oth[...] = keys(lambda q: norm_oth[q])
    key_copy = send(key_oth, key_in, other_core)

    c_copies = [[None] * SIDE, [None] * SIDE]

    def combine(i):
        for hf in range(2):
            a = at1[hf] + rel[i] + SIDE
            copies = []
            for d in range(2):
                e_copies[hf][i][d].wait_recv()
                where = cut(block(hf, a, at2[hf] + STEP[d] + SIDE), SIDE_COLS[d])
                part_bf[where] = (part[where] + e_in[hf, d, i].astype(F32)).astype(BF16)
                copies.append(send(part_bf.at[where], s_in.at[hf, d, i, :, SIDE_COLS[d]], along(second[hf], STEP[d])))
            c_copies[hf][i] = copies

    for i in order:
        combine(i)

    key_own[...] = keys(lambda q: norm[q, core])

    for copy in rep_copies:
        copy.wait_recv()
    pseudo_ref[...] = (
        diffs[0].astype(F32) + diffs[1].astype(F32) + diffs[2].astype(F32) + diffs[3].astype(F32)) / REPS

    key_copy.wait_recv()
    key_ref[...] = (key_own[...] + key_in[...]).astype(BF16)

    e2_copies = [None, None]
    d2_copies = [[None, None], [None, None]]
    for i in order:
        for hf in range(2):
            for d in range(2):
                c_copies[hf][i][d].wait_recv()
                d_copies[hf][i][d].wait_recv()
            a = at1[hf] + rel[i] + SIDE
            total = part[block(hf, a, at2[hf])] + s_in[hf, 0, i].astype(F32) + s_in[hf, 1, i].astype(F32)
            s_sum[hf, i] = total
            s_bf[hf, i] = total.astype(BF16)
            if i == 3:
                e2_copies[hf] = [
                    send(s_bf.at[hf, i, :, SIDE_COLS[d]], e2_in.at[hf, d], along(first[hf], STEP[d])) for d in range(2)]
            elif i > 0:
                d = 2 - i
                d2_copies[hf][d] = send(
                    s_bf.at[hf, i, :, SIDE_COLS[1 - d]], s2_in.at[hf, d, :, SIDE_COLS[1 - d]], along(first[hf], STEP[d]))

    c2_copies = [[None, None], [None, None]]
    for hf in range(2):
        for d in range(2):
            i = 2 - d
            e2_copies[hf][d].wait_recv()
            s_bf[hf, i, :, SIDE_COLS[d]] = (s_sum[hf, i, :, SIDE_COLS[d]] + e2_in[hf, d].astype(F32)).astype(BF16)
            c2_copies[hf][d] = send(
                s_bf.at[hf, i, :, SIDE_COLS[d]], s2_in.at[hf, d, :, SIDE_COLS[d]], along(first[hf], STEP[d]))
    for hf in range(2):
        for d in range(2):
            c2_copies[hf][d].wait_recv()
            d2_copies[hf][d].wait_recv()
        total = s_sum[hf, 0] + s2_in[hf, 0].astype(F32) + s2_in[hf, 1].astype(F32)
        t_sum[hf] = total
        t_bf[hf] = total.astype(BF16)

    z_near, z_far0, z_far1 = slot(), slot(), slot()
    z_got = (slot(), slot())

    @pl.when(home)
    def _():
        push(t_bf.at[1 - core], z_in.at[0], other_core, z_near, z_got[0])

    @pl.when(jnp.logical_not(home))
    def _():
        push(t_bf.at[0], z_in.at[1], dev(y, core, x, 0), z_far0, z_got[1])
        push(t_bf.at[1], z_in.at[1], dev(y, core, x, 1), z_far1, z_got[1])

    def z_copy(sem, got):
        return pltpu.make_async_remote_copy(
            src_ref=t_bf.at[0], dst_ref=z_in.at[0], send_sem=send_sem.at[sem], recv_sem=recv_sem.at[got],
            device_id=other_core, device_id_type=MESH)

    z_copy(z_far0, z_got[1]).wait_recv()

    @pl.when(home)
    def _():
        grad_ref[...] = t_sum[core] + z_in[1].astype(F32)

    @pl.when(jnp.logical_not(home))
    def _():
        z_copy(z_near, z_got[0]).wait_recv()
        grad_ref[...] = z_in[0].astype(F32) + z_in[1].astype(F32)

    far_copy.wait_send()

    @pl.when(home)
    def _():
        z_copy(z_near, z_got[0]).wait_send()

    @pl.when(jnp.logical_not(home))
    def _():
        z_copy(w_near, z_got[0]).wait_send()
        z_copy(z_far0, z_got[0]).wait_send()
        z_copy(z_far1, z_got[0]).wait_send()

    for copy in started:
        copy.wait_send()


def exchange(tokens, gain, master, cot, frag_global, frag_local, index):
    n_tok, width = tokens.shape
    rows, cols = master.shape
    n_group = SIDE * PLANES
    group = width // n_group
    half = cols // 2
    any_spec = pl.BlockSpec(memory_space=pl.ANY)
    vmem_spec = pl.BlockSpec(memory_space=pltpu.VMEM)
    return pl.pallas_call(
        kernel,
        out_shape=(
            jax.ShapeDtypeStruct((n_tok, cols), BF16),
            jax.ShapeDtypeStruct((rows, cols), F32),
            jax.ShapeDtypeStruct((rows, cols), F32),
        ),
        in_specs=[any_spec] * 6 + [pl.BlockSpec(memory_space=pltpu.SMEM)],
        out_specs=(vmem_spec,) * 3,
        scratch_shapes=[
            pltpu.VMEM((n_tok, width), BF16),
            pltpu.VMEM((1, width), F32),
            pltpu.VMEM((rows, cols), F32),
            pltpu.VMEM(frag_global.shape, F32),
            pltpu.VMEM(frag_local.shape, F32),
            pltpu.VMEM((n_tok, cols), BF16),
            pltpu.VMEM((n_tok, cols), BF16),
            pltpu.VMEM((rows, cols), BF16),
            pltpu.VMEM((SIDE, group, cols), BF16),
            pltpu.VMEM((SIDE, PLANES, n_tok, group), BF16),
            pltpu.VMEM((SIDE, n_tok, group), BF16),
            pltpu.VMEM((SIDE, group, cols), F32),
            pltpu.VMEM((SIDE, group, cols), BF16),
            pltpu.VMEM((2, 2, SIDE, rows, half), BF16),
            pltpu.VMEM((2, 2, SIDE, rows, cols), BF16),
            pltpu.VMEM((2, SIDE, rows, cols), F32),
            pltpu.VMEM((2, SIDE, rows, cols), BF16),
            pltpu.VMEM((2, 2, rows, half), BF16),
            pltpu.VMEM((2, 2, rows, cols), BF16),
            pltpu.VMEM((2, rows, cols), F32),
            pltpu.VMEM((2, rows, cols), BF16),
            pltpu.VMEM((2, rows, cols), BF16),
            pltpu.VMEM((n_tok, cols), F32),
            pltpu.VMEM((n_tok, cols), F32),
            pltpu.VMEM((n_tok, cols), F32),
            pltpu.VMEM((REPS, rows, cols), BF16),
            pltpu.SemaphoreType.DMA((12,)),
            pltpu.SemaphoreType.DMA((N_SEMS,)),
            pltpu.SemaphoreType.DMA((N_SEMS,)),
        ],
        compiler_params=pltpu.CompilerParams(
            collective_id=0, has_side_effects=True, vmem_limit_bytes=60 * 1024 * 1024
        ),
        cost_estimate=pl.CostEstimate(flops=4 * n_tok * width * cols, bytes_accessed=10 * 1024 * 1024, transcendentals=0),
    )(tokens, gain, master, cot, frag_global, frag_local, index)


def shards(
    tokens,
    norm_gain,
    master_weight,
    inner_moment,
    inner_second,
    cotangent,
    frag_global,
    frag_local,
    outer_momentum,
    fragment_index,
):
    master = master_weight[0]
    key_rows, grad, pseudo_grad = exchange(
        tokens[0], norm_gain[None], master, cotangent[0], frag_global, frag_local[0], fragment_index)
    moment_next = 0.9 * inner_moment[0] + 0.1 * grad
    second_next = 0.95 * inner_second[0] + 0.05 * grad * grad
    master_next = master - 0.02 * (moment_next / (jnp.sqrt(second_next) + 1e-08) + 0.1 * master)
    frag_total = frag_global.shape[0]
    outer_step = fragment_index[0]
    frag_pick = outer_step % frag_total
    round_count = (outer_step // frag_total).astype(jnp.float32)
    outer_rate = 0.7 * (1.0 - round_count / 512.0)
    frag_now = lax.dynamic_index_in_dim(frag_global, frag_pick, 0, keepdims=False)
    moment_now = lax.dynamic_index_in_dim(outer_momentum, frag_pick, 0, keepdims=False)
    new_outer = 0.9 * moment_now + pseudo_grad
    new_global = frag_now - outer_rate * (pseudo_grad + 0.9 * new_outer)
    return (
        key_rows[None],
        master_next[None],
        moment_next[None],
        second_next[None],
        new_global,
        new_outer,
    )


def solution(mesh):
    in_specs = (
        P("rep", "fsdp", None),
        P(),
        P("rep", "fsdp", None),
        P("rep", "fsdp", None),
        P("rep", "fsdp", None),
        P("rep", "fsdp", None),
        P(None, "fsdp", None),
        P("rep", None, "fsdp", None),
        P(None, "fsdp", None),
        P(),
    )
    out_specs = (
        P("rep", "fsdp", None),
        P("rep", "fsdp", None),
        P("rep", "fsdp", None),
        P("rep", "fsdp", None),
        P("fsdp", None),
        P("fsdp", None),
    )
    return jax.shard_map(shards, mesh=mesh, in_specs=in_specs, out_specs=out_specs, check_vma=False)
```

time: 461 us -> 81.7 us (0.18); the launches traced: 456 us -> 81.5 us
  waiting for transfers between devices: 410 us -> 0 us
  Pallas kernels: 0 us -> 74.5 us
  matrix products: 19 us -> 0 us
  between operations: 16.2 us -> 1.39 us
  other arithmetic: 10.8 us -> 3.93 us
    reduce_scatter x1 -> x0, waiting for transfers between devices: 304 us -> none  [shards(): lax.psum_scatter(lax.dot_general(feature_cols, upstream, (((0,), (0,)), (...]
    pallas_call x0 -> x1, Pallas kernels: none -> 74.5 us  [exchange(): pl.pallas_call(kernel, out_shape=(jax.ShapeDtypeStruct((n_tok, cols), BF1...]
    all_gather x1 -> x0, waiting for transfers between devices: 65.8 us -> none  [shards(): lax.all_gather(weight_bf, 'fsdp', axis=0, tiled=True)]
    psum x1 -> x0, waiting for transfers between devices: 40 us -> none  [shards(): pseudo_grad = lax.psum(pseudo_local, 'rep') / replicas]
    dot_general x2 -> x0, matrix products: 19 us -> none  [the longest x1 10.5 us: shards(): lax.dot_general(feature_cols, upstream, (((0,), (0,)), ((), ())), preferr...]
  transfers between devices with their start and end apart: 3 -> 0, of which waited for: 3 -> 0; matrix products, arithmetic and copies ran while one was open for 6% -> 0% of each run, Pallas kernels for 0% -> 0%
where the time goes in v1:
time: 81.7 us; the launch traced here: 81.5 us
  Pallas kernels  74.5 us (91%)
  other arithmetic  3.93 us (5%)
  local copies, waits for them, and re-layouts  1.69 us (2%)
  between operations  1.39 us (2%)
    pallas_call x1, Pallas kernels, exchange(): pl.pallas_call(kernel, out_shape=(jax.ShapeDtypeStruct((n_tok, cols), BF1...  74.5 us
    broadcast_in_dim x1, other arithmetic, shards(): second_next[None]  2.07 us
    sub x1, other arithmetic, shards(): new_global = frag_now - outer_rate * (pseudo_grad + 0.9 * new_outer)  1.86 us
    unnamed x11, local copies, waits for them, and re-layouts  1.69 us

profile of v1, /device:TPU:1, one launch (start us, length us, event | category | flops | bytes accessed | tf_op | source)
XLA Modules:
  0.0 81.5 jit_solution(15396311717683404981)
XLA Ops:
  1.3 0.0 copy-start.3
  1.3 0.0 copy-start.4
  1.3 0.0 copy-start
  1.3 0.0 copy-start.1
  1.4 0.0 copy-start.2
  1.4 74.5 %shard_map.145 = (bf16[256,512]{1,0:T(8,128)(2,1)}, f32[144,512]{1,0:T(8,128)}, f32[144,512]{1,0:T(8,128)}) custom-call(bf16[256,9216]{1,0:T(8,128)(2,1)} %bitcast.37, f32[1,9216]{1,0:T(1,128)} %bitcast.40, f32[144,512]{1,0:T(8,128)} %bitcast.35, bf16[256,512]{1,0:T(8,128)(2,1)} %bitcast.39, f32[2,144,512]{2,1,0:T(8,128)} %global_hbm.1, ...), custom_call_target="tpu_custom_call" | custom-call | flops 4831838208 | bytes 10485760 | tf_op jit(solution)/shard_map/pallas_call | solution.py:383
  75.8 0.0 copy-done.3
  75.8 0.0 copy-done.4
  75.9 1.9 %bitcast_subtract_fusion = (f32[144,512]{1,0:T(8,128)}, f32[144,512]{1,0:T(8,128)}) fusion(f32[144,512]{1,0:T(8,128)} %get-tuple-element.11, f32[2,144,512]{2,1,0:T(8,128)S(1)} %copy-done.3, s32[]{:T(128)S(6)} %select_n.17, f32[]{:T(128)S(6)} %mul_shard_map.3, f32[2,144,512]{2,1,0:T(8,128)S(1)} %copy-done.4), kind=kLoop, calls=%fused_computation.3 | loop fusion | flops 442368 | bytes 1474568 | tf_op jit(solution)/shard_map/sub | solution.py:456
  77.7 0.0 copy-done
  77.7 0.0 copy-done.1
  77.7 0.0 copy-done.2
  77.7 2.1 %fusion.2 = (f32[1,144,512]{2,1,0:T(8,128)}, f32[1,144,512]{2,1,0:T(8,128)}, f32[1,144,512]{2,1,0:T(8,128)}) fusion(f32[144,512]{1,0:T(8,128)} %get-tuple-element.10, f32[1,144,512]{2,1,0:T(8,128)S(1)} %copy-done.1, f32[1,144,512]{2,1,0:T(8,128)S(1)} %copy-done.2, f32[1,144,512]{2,1,0:T(8,128)S(1)} %copy-done), kind=kLoop, calls=%fused_computation.7 | loop fusion | flops 958464 | bytes 2064384 | tf_op jit(solution)/shard_map/broadcast_in_dim | solution.py:461
  79.8 1.7 %copy.18 = bf16[1,256,512]{2,1,0:T(8,128)(2,1)} copy(bf16[1,256,512]{2,1,0:T(8,128)(2,1)} %bitcast.36) | data formatting | bytes 524288
Async XLA Ops:
  1.3 74.5 %copy-start.3 = (f32[2,144,512]{2,1,0:T(8,128)S(1)}, f32[2,144,512]{2,1,0:T(8,128)}, u32[]{:S(2)}) copy-start(f32[2,144,512]{2,1,0:T(8,128)} %global_hbm.1) | copy-start | bytes 1769476
  1.3 74.5 %copy-start.4 = (f32[2,144,512]{2,1,0:T(8,128)S(1)}, f32[2,144,512]{2,1,0:T(8,128)}, u32[]{:S(2)}) copy-start(f32[2,144,512]{2,1,0:T(8,128)} %param.18) | copy-start | bytes 1769476
  1.3 76.4 %copy-start = (f32[1,144,512]{2,1,0:T(8,128)S(1)}, f32[1,144,512]{2,1,0:T(8,128)}, u32[]{:S(2)}) copy-start(f32[1,144,512]{2,1,0:T(8,128)} %param.12) | copy-start | bytes 884740
  1.3 76.4 %copy-start.1 = (f32[1,144,512]{2,1,0:T(8,128)S(1)}, f32[1,144,512]{2,1,0:T(8,128)}, u32[]{:S(2)}) copy-start(f32[1,144,512]{2,1,0:T(8,128)} %param.14) | copy-start | bytes 884740
  1.4 76.4 %copy-start.2 = (f32[1,144,512]{2,1,0:T(8,128)S(1)}, f32[1,144,512]{2,1,0:T(8,128)}, u32[]{:S(2)}) copy-start(f32[1,144,512]{2,1,0:T(8,128)} %param.13) | copy-start | bytes 884740

commit v2 on v1

--- a/solution.py
+++ b/solution.py
@@ -12,9 +12,10 @@
 BF16 = jnp.bfloat16
 REPS = 4
 SIDE = 4
+NFRAG = 2
 PLANES = 2
 STRIP = 32
-N_SEMS = 160
+N_SEMS = 192
 
 
 def kernel(
@@ -22,7 +23,7 @@
     key_ref, grad_ref, pseudo_ref,
     tok, gain, master, frag_now, frag_local, cot, cot_oth,
     w_own, w, norm, norm_oth, part, part_bf, e_in, s_in, s_sum, s_bf, e2_in, s2_in,
-    t_sum, t_bf, z_in, key_own, key_oth, key_in, diffs,
+    t_sum, t_bf, z_in, key_own, key_oth, key_in, diffs, r_in, r_sum,
     in_sem, send_sem, recv_sem,
 ):
     rows, cols = master.shape
@@ -72,6 +73,15 @@
         copy = push(src, dst, to)
         started.append(copy)
         return copy
+
+    named = {}
+
+    def remote(name, src, dst, to):
+        if name not in named:
+            named[name] = slot()
+        return pltpu.make_async_remote_copy(
+            src_ref=src, dst_ref=dst, send_sem=send_sem.at[named[name]], recv_sem=recv_sem.at[named[name]],
+            device_id=to, device_id_type=MESH)
 
     loads = []
 
@@ -143,8 +153,15 @@
                 v = v * inverse * gain[:, t * 128:(t + 1) * 128]
                 norm[g // PLANES, g % PLANES, at, l * 128:(l + 1) * 128] = v.astype(BF16)
 
+    def swap(i):
+        at = pl.ds(i * chunk, chunk)
+        return send(norm.at[:, 1 - core, at], norm_oth.at[:, at], other_core)
+
     load_gain.wait()
-    normalise(0)
+    norm_copies = []
+    for i in range(n_chunk - 1):
+        normalise(i)
+        norm_copies.append(swap(i))
 
     first, second = ("x", "y"), ("y", "x")
     at1, at2 = (x, y), (y, x)
@@ -165,42 +182,116 @@
                 src_ref=w_own, dst_ref=own_at, send_sem=send_sem.at[w_far], recv_sem=recv_sem.at[w_got[c_]],
                 device_id=other_core, device_id_type=MESH).wait_recv()
 
-    def gather_second(hf, a):
-        ref = w.at[block(hf, a, at2[hf])]
-        return [send(ref, ref, along(second[hf], STEP[d])) for d in range(2)]
-
-    def gather_forward(hf, copies, a):
-        out = []
+    rel = (0, -1, 1, 2)
+    FULL = (pl.ds(0, cols), lo)
+    SIDES = ((lo, hi), (pl.ds(0, half // 2), pl.ds(half // 2, half // 2)))
+
+    def piece_of(hf, i, j, columns):
+        return w.at[cut(block(hf, at1[hf] + rel[i] + SIDE, at2[hf] + rel[j] + SIDE), columns)]
+
+    def g1(role, hf, d):
+        ref = piece_of(hf, 0, 0, FULL[role])
+        return remote((1, hf, d), ref, ref, along(first[hf], STEP[d]))
+
+    def g1f(role, hf, d):
+        ref = piece_of(hf, 1 + d, 0, SIDES[role][d])
+        return remote((2, hf, d), ref, ref, along(first[hf], STEP[d]))
+
+    def g2(role, hf, i, d):
+        ref = piece_of(hf, i, 0, FULL[role])
+        return remote((3, hf, i, d), ref, ref, along(second[hf], STEP[d]))
+
+    def g2f(role, hf, i, d):
+        ref = piece_of(hf, i, 1 + d, SIDES[role][d])
+        return remote((4, hf, i, d), ref, ref, along(second[hf], STEP[d]))
+
+    def gz(hf, i, j):
+        ref = piece_of(hf, i, j, hi)
+        return remote((5, hf, i, j), ref, ref, dev(y, 1 - z, x, core))
+
+    def each_role(step):
+        @pl.when(home)
+        def _():
+            step(0)
+
+        @pl.when(jnp.logical_not(home))
+        def _():
+            step(1)
+
+    def gather_start(role):
+        for hf in range(2):
+            for d in range(2):
+                g1(role, hf, d).start()
+        for hf in range(2):
+            for d in range(2):
+                g2(role, hf, 0, d).start()
+
+    def gather_first(role):
+        for hf in range(2):
+            for d in range(2):
+                g1(role, hf, d).wait_recv()
+                g1f(role, hf, d).start()
+                for d2 in range(2):
+                    g2(role, hf, 1 + d, d2).start()
+                if role == 0:
+                    gz(hf, 1 + d, 0).start()
+
+    def gather_turn(role):
+        for hf in range(2):
+            gather_on(role, hf, 0)
+            for d in range(2):
+                g1f(role, hf, d).wait_recv()
+            for d in range(2):
+                g2(role, hf, 3, d).start()
+            if role == 0:
+                gz(hf, 3, 0).start()
+
+    def gather_on(role, hf, i):
         for d in range(2):
-            copies[d].wait_recv()
-            ref = w.at[cut(block(hf, a, at2[hf] - STEP[d] + SIDE), SIDE_COLS[d])]
-            out.append(send(ref, ref, along(second[hf], STEP[d])))
-        return out
-
-    one = []
-    for hf in range(2):
-        ref = w.at[block(hf, at1[hf], at2[hf])]
-        one.append([send(ref, ref, along(first[hf], STEP[d])) for d in range(2)])
-    two = [[gather_second(hf, at1[hf])] for hf in range(2)]
-
-    for i in range(1, n_chunk):
-        normalise(i)
-    norm_copies = [send(norm.at[q, 1 - core], norm_oth.at[q], other_core) for q in range(SIDE)]
+            g2(role, hf, i, d).wait_recv()
+            g2f(role, hf, i, d).start()
+            if role == 0:
+                gz(hf, i, 1 + d).start()
+
+    def gather_last(role, i):
+        for hf in range(2):
+            for d in range(2):
+                g2f(role, hf, i, d).wait_recv()
+            if role == 0:
+                gz(hf, i, 3).start()
+
+    def gather_all(role, done):
+        for hf in range(2):
+            for d in range(2):
+                getattr(g1(role, hf, d), done)()
+                getattr(g1f(role, hf, d), done)()
+                for i in range(SIDE):
+                    getattr(g2(role, hf, i, d), done)()
+                    getattr(g2f(role, hf, i, d), done)()
+
+    def gather_far(done):
+        for hf in range(2):
+            for i in range(SIDE):
+                for j in range(SIDE):
+                    if i or j:
+                        getattr(gz(hf, i, j), done)()
+
+    each_role(gather_start)
+
+    normalise(n_chunk - 1)
+    norm_copies.append(swap(n_chunk - 1))
 
     load_now.wait()
     load_loc.wait()
     k = index_ref[0] % frag_now.shape[0]
-    diffs[rep] = (frag_now[k] - frag_local[k]).astype(BF16)
-    rep_copies = [send(diffs.at[rep], diffs.at[rep], {"rep": (rep + j) % REPS}) for j in range(1, REPS)]
-
-    one_f = [[None, None], [None, None]]
-    for hf in range(2):
-        for d in range(2):
-            one[hf][d].wait_recv()
-            a = at1[hf] - STEP[d] + SIDE
-            ref = w.at[cut(block(hf, a, at2[hf]), SIDE_COLS[d])]
-            one_f[hf][d] = send(ref, ref, along(first[hf], STEP[d]))
-            two[hf].append(gather_second(hf, a))
+    diffs[...] = (frag_now[k] - frag_local[k]).astype(BF16)
+    quarter = cols // REPS
+
+    def quarter_of(r):
+        return diffs.at[:, pl.ds(pl.multiple_of(r * quarter, quarter), quarter)]
+
+    r_in[rep] = diffs[:, pl.ds(pl.multiple_of(rep * quarter, quarter), quarter)]
+    rep_copies = [send(quarter_of((rep + j) % REPS), r_in.at[rep], {"rep": (rep + j) % REPS}) for j in range(1, REPS)]
 
     piece = group // 3
     over_tokens = (((0,), (0,)), ((), ()))
@@ -211,13 +302,7 @@
             part[q, j * piece:(j + 1) * piece, :] = lax.dot_general(
                 norm[q, core, :, j * piece:(j + 1) * piece], cot[...], over_tokens, preferred_element_type=F32)
 
-    two_f = [[None] * SIDE, [None] * SIDE]
-    for hf in range(2):
-        two_f[hf][0] = gather_forward(hf, two[hf][0], at1[hf])
-    for hf in range(2):
-        for d in range(2):
-            one_f[hf][d].wait_recv()
-        two[hf].append(gather_second(hf, at1[hf] + 2))
+    each_role(gather_first)
 
     cot_copy.wait_recv()
     for copy in norm_copies:
@@ -231,20 +316,17 @@
             part[q, j * piece:(j + 1) * piece, :] = total
             part_bf[q, j * piece:(j + 1) * piece, :] = total.astype(BF16)
 
-    rel = (0, -1, 1, 2)
-    for hf in range(2):
-        for i in range(1, SIDE):
-            two_f[hf][i] = gather_forward(hf, two[hf][i], at1[hf] + rel[i] + SIDE)
-
     order = (3, 2, 1, 0)
     e_copies = [[None] * SIDE, [None] * SIDE]
     d_copies = [[None] * SIDE, [None] * SIDE]
+    c_copies = [[None] * SIDE, [None] * SIDE]
     for i in order:
         for hf in range(2):
             a = at1[hf] + rel[i] + SIDE
             e_copies[hf][i] = [
                 send(part_bf.at[cut(block(hf, a, at2[hf] + 2), SIDE_COLS[d])], e_in.at[hf, d, i], along(second[hf], STEP[d]))
                 for d in range(2)]
+    each_role(gather_turn)
     for i in order:
         for hf in range(2):
             a = at1[hf] + rel[i] + SIDE
@@ -253,22 +335,6 @@
                      s_in.at[hf, d, i, :, SIDE_COLS[1 - d]], along(second[hf], STEP[d]))
                 for d in range(2)]
 
-    for hf in range(2):
-        for i in range(SIDE):
-            for copy in two_f[hf][i]:
-                copy.wait_recv()
-
-    def keys(operand):
-        total = jnp.dot(operand(0), w[0], preferred_element_type=F32)
-        for q in range(1, SIDE):
-            total = total + jnp.dot(operand(q), w[q], preferred_element_type=F32)
-        return total
-
-    key_oth[...] = keys(lambda q: norm_oth[q])
-    key_copy = send(key_oth, key_in, other_core)
-
-    c_copies = [[None] * SIDE, [None] * SIDE]
-
     def combine(i):
         for hf in range(2):
             a = at1[hf] + rel[i] + SIDE
@@ -280,30 +346,19 @@
                 copies.append(send(part_bf.at[where], s_in.at[hf, d, i, :, SIDE_COLS[d]], along(second[hf], STEP[d])))
             c_copies[hf][i] = copies
 
-    for i in order:
-        combine(i)
-
-    key_own[...] = keys(lambda q: norm[q, core])
-
-    for copy in rep_copies:
-        copy.wait_recv()
-    pseudo_ref[...] = (
-        diffs[0].astype(F32) + diffs[1].astype(F32) + diffs[2].astype(F32) + diffs[3].astype(F32)) / REPS
-
-    key_copy.wait_recv()
-    key_ref[...] = (key_own[...] + key_in[...]).astype(BF16)
-
     e2_copies = [None, None]
     d2_copies = [[None, None], [None, None]]
-    for i in order:
-        for hf in range(2):
-            for d in range(2):
+
+    def settle(i):
+        for hf in range(2):
+            for d in range(2):
+                d_copies[hf][i][d].wait_recv()
                 c_copies[hf][i][d].wait_recv()
-                d_copies[hf][i][d].wait_recv()
             a = at1[hf] + rel[i] + SIDE
             total = part[block(hf, a, at2[hf])] + s_in[hf, 0, i].astype(F32) + s_in[hf, 1, i].astype(F32)
             s_sum[hf, i] = total
-            s_bf[hf, i] = total.astype(BF16)
+            if i > 0:
+                s_bf[hf, i] = total.astype(BF16)
             if i == 3:
                 e2_copies[hf] = [
                     send(s_bf.at[hf, i, :, SIDE_COLS[d]], e2_in.at[hf, d], along(first[hf], STEP[d])) for d in range(2)]
@@ -311,6 +366,32 @@
                 d = 2 - i
                 d2_copies[hf][d] = send(
                     s_bf.at[hf, i, :, SIDE_COLS[1 - d]], s2_in.at[hf, d, :, SIDE_COLS[1 - d]], along(first[hf], STEP[d]))
+
+    def on(i):
+        each_role(lambda role: [gather_on(role, hf, i) for hf in range(2)])
+
+    def last(i):
+        each_role(lambda role: gather_last(role, i))
+
+    combine(3)
+    combine(2)
+    on(1)
+    on(2)
+
+    for copy in rep_copies:
+        copy.wait_recv()
+    r_sum[rep] = (r_in[0].astype(F32) + r_in[1].astype(F32) + r_in[2].astype(F32) + r_in[3].astype(F32)).astype(BF16)
+    sum_copies = [send(r_sum.at[rep], r_sum.at[rep], {"rep": (rep + j) % REPS}) for j in range(1, REPS)]
+
+    combine(1)
+    settle(3)
+    on(3)
+    last(0)
+    combine(0)
+    last(1)
+    last(2)
+    settle(2)
+    settle(1)
 
     c2_copies = [[None, None], [None, None]]
     for hf in range(2):
@@ -320,6 +401,10 @@
             s_bf[hf, i, :, SIDE_COLS[d]] = (s_sum[hf, i, :, SIDE_COLS[d]] + e2_in[hf, d].astype(F32)).astype(BF16)
             c2_copies[hf][d] = send(
                 s_bf.at[hf, i, :, SIDE_COLS[d]], s2_in.at[hf, d, :, SIDE_COLS[d]], along(first[hf], STEP[d]))
+
+    last(3)
+
+    settle(0)
     for hf in range(2):
         for d in range(2):
             c2_copies[hf][d].wait_recv()
@@ -340,6 +425,27 @@
         push(t_bf.at[0], z_in.at[1], dev(y, core, x, 0), z_far0, z_got[1])
         push(t_bf.at[1], z_in.at[1], dev(y, core, x, 1), z_far1, z_got[1])
 
+    @pl.when(jnp.logical_not(home))
+    def _():
+        gather_far("wait_recv")
+
+    def keys(operand):
+        total = jnp.dot(operand(0), w[0], preferred_element_type=F32)
+        for q in range(1, SIDE):
+            total = total + jnp.dot(operand(q), w[q], preferred_element_type=F32)
+        return total
+
+    key_oth[...] = keys(lambda q: norm_oth[q])
+    key_copy = send(key_oth, key_in, other_core)
+    key_own[...] = keys(lambda q: norm[q, core])
+    key_copy.wait_recv()
+    key_ref[...] = (key_own[...] + key_in[...]).astype(BF16)
+
+    for copy in sum_copies:
+        copy.wait_recv()
+    for r in range(REPS):
+        pseudo_ref[:, r * quarter:(r + 1) * quarter] = r_sum[r].astype(F32) / REPS
+
     def z_copy(sem, got):
         return pltpu.make_async_remote_copy(
             src_ref=t_bf.at[0], dst_ref=z_in.at[0], send_sem=send_sem.at[sem], recv_sem=recv_sem.at[got],
@@ -367,6 +473,12 @@
         z_copy(w_near, z_got[0]).wait_send()
         z_copy(z_far0, z_got[0]).wait_send()
         z_copy(z_far1, z_got[0]).wait_send()
+
+    each_role(lambda role: gather_all(role, "wait_send"))
+
+    @pl.when(home)
+    def _():
+        gather_far("wait_send")
 
     for copy in started:
         copy.wait_send()
@@ -415,7 +527,9 @@
             pltpu.VMEM((n_tok, cols), F32),
             pltpu.VMEM((n_tok, cols), F32),
             pltpu.VMEM((n_tok, cols), F32),
-            pltpu.VMEM((REPS, rows, cols), BF16),
+            pltpu.VMEM((rows, cols), BF16),
+            pltpu.VMEM((REPS, rows, cols // REPS), BF16),
+            pltpu.VMEM((REPS, rows, cols // REPS), BF16),
             pltpu.SemaphoreType.DMA((12,)),
             pltpu.SemaphoreType.DMA((N_SEMS,)),
             pltpu.SemaphoreType.DMA((N_SEMS,)),
@@ -425,6 +539,46 @@
         ),
         cost_estimate=pl.CostEstimate(flops=4 * n_tok * width * cols, bytes_accessed=10 * 1024 * 1024, transcendentals=0),
     )(tokens, gain, master, cot, frag_global, frag_local, index)
+
+
+def update_kernel(
+    index_ref, key_in, grad_in, pseudo_in, master, moment, second, frag_now, momentum,
+    key_out, master_out, moment_out, second_out, global_out, outer_out,
+):
+    key_out[...] = key_in[...]
+    grad = grad_in[...]
+    moment_next = 0.9 * moment[...] + 0.1 * grad
+    second_next = 0.95 * second[...] + 0.05 * grad * grad
+    old = master[...]
+    moment_out[...] = moment_next
+    second_out[...] = second_next
+    master_out[...] = old - 0.02 * (moment_next / (jnp.sqrt(second_next) + 1e-08) + 0.1 * old)
+    round_count = (index_ref[0] // NFRAG).astype(F32)
+    outer_rate = 0.7 * (1.0 - round_count / 512.0)
+    pseudo = pseudo_in[...]
+    new_outer = 0.9 * momentum[...] + pseudo
+    outer_out[...] = new_outer
+    global_out[...] = frag_now[...] - outer_rate * (pseudo + 0.9 * new_outer)
+
+
+def update(index, key_rows, grad, pseudo, master, moment, second, frag_global, momentum):
+    steps = 2
+    rows, cols = grad.shape
+    n_tok = key_rows.shape[0]
+    key_spec = pl.BlockSpec((n_tok // steps, cols), lambda i, index: (i, 0))
+    row_spec = pl.BlockSpec((rows // steps, cols), lambda i, index: (i, 0))
+    frag_spec = pl.BlockSpec((None, rows // steps, cols), lambda i, index: (index[0] % NFRAG, i, 0))
+    rows_f32 = jax.ShapeDtypeStruct((rows, cols), F32)
+    return pl.pallas_call(
+        update_kernel,
+        out_shape=(jax.ShapeDtypeStruct(key_rows.shape, BF16),) + (rows_f32,) * 5,
+        grid_spec=pltpu.PrefetchScalarGridSpec(
+            num_scalar_prefetch=1,
+            grid=(steps,),
+            in_specs=[key_spec] + [row_spec] * 5 + [frag_spec] * 2,
+            out_specs=(key_spec,) + (row_spec,) * 5,
+        ),
+    )(index, key_rows, grad, pseudo, master, moment, second, frag_global, momentum)
 
 
 def shards(
@@ -442,18 +596,8 @@
     master = master_weight[0]
     key_rows, grad, pseudo_grad = exchange(
         tokens[0], norm_gain[None], master, cotangent[0], frag_global, frag_local[0], fragment_index)
-    moment_next = 0.9 * inner_moment[0] + 0.1 * grad
-    second_next = 0.95 * inner_second[0] + 0.05 * grad * grad
-    master_next = master - 0.02 * (moment_next / (jnp.sqrt(second_next) + 1e-08) + 0.1 * master)
-    frag_total = frag_global.shape[0]
-    outer_step = fragment_index[0]
-    frag_pick = outer_step % frag_total
-    round_count = (outer_step // frag_total).astype(jnp.float32)
-    outer_rate = 0.7 * (1.0 - round_count / 512.0)
-    frag_now = lax.dynamic_index_in_dim(frag_global, frag_pick, 0, keepdims=False)
-    moment_now = lax.dynamic_index_in_dim(outer_momentum, frag_pick, 0, keepdims=False)
-    new_outer = 0.9 * moment_now + pseudo_grad
-    new_global = frag_now - outer_rate * (pseudo_grad + 0.9 * new_outer)
+    key_rows, master_next, moment_next, second_next, new_global, new_outer = update(
+        fragment_index, key_rows, grad, pseudo_grad, master, inner_moment[0], inner_second[0], frag_global, outer_momentum)
     return (
         key_rows[None],
         master_next[None],

time: 81.7 us -> 71.5 us (0.88)
  Pallas kernels: 74.5 us -> 69.4 us
  other arithmetic: 3.93 us -> 0 us
  local copies, waits for them, and re-layouts: 1.69 us -> 0 us
    pallas_call x1, Pallas kernels: 74.5 us -> 66.7 us  [exchange(): pl.pallas_call(kernel, out_shape=(jax.ShapeDtypeStruct((n_tok, cols), BF1...]
    pallas_call x0 -> x1, Pallas kernels: none -> 2.7 us  [update(): pl.pallas_call(update_kernel, out_shape=(jax.ShapeDtypeStruct(key_rows.sh...]
    broadcast_in_dim x1 -> x0, other arithmetic: 2.07 us -> none  [shards(): second_next[None]]
    sub x1 -> x0, other arithmetic: 1.86 us -> none  [shards(): new_global = frag_now - outer_rate * (pseudo_grad + 0.9 * new_outer)]
    unnamed x11 -> x0, local copies, waits for them, and re-layouts: 1.69 us -> none
where the time goes in v2:
time: 71.5 us; the launch traced here: 70.7 us
  Pallas kernels  69.4 us (97%)
  between operations  1.29 us (2%)
    pallas_call x1, Pallas kernels, exchange(): pl.pallas_call(kernel, out_shape=(jax.ShapeDtypeStruct((n_tok, cols), BF1...  66.7 us
    pallas_call x1, Pallas kernels, update(): pl.pallas_call(update_kernel, out_shape=(jax.ShapeDtypeStruct(key_rows.sh...  2.7 us

profile of v2, /device:TPU:1, one launch (start us, length us, event | category | flops | bytes accessed | tf_op | source)
XLA Modules:
  0.0 70.7 jit_solution(148698344167930382)
XLA Ops:
  1.3 66.7 %shard_map.145 = (bf16[256,512]{1,0:T(8,128)(2,1)}, f32[144,512]{1,0:T(8,128)}, f32[144,512]{1,0:T(8,128)}) custom-call(bf16[256,9216]{1,0:T(8,128)(2,1)} %bitcast.15, f32[1,9216]{1,0:T(1,128)} %bitcast.22, f32[144,512]{1,0:T(8,128)} %bitcast.11, bf16[256,512]{1,0:T(8,128)(2,1)} %bitcast.20, f32[2,144,512]{2,1,0:T(8,128)} %frag_now.1, ...), custom_call_target="tpu_custom_call" | custom-call | flops 4831838208 | bytes 10485760 | tf_op jit(solution)/shard_map/pallas_call | solution.py:495
  68.0 2.7 %shard_map.146 = (bf16[256,512]{1,0:T(8,128)(2,1)}, f32[144,512]{1,0:T(8,128)}, f32[144,512]{1,0:T(8,128)}, f32[144,512]{1,0:T(8,128)}, f32[144,512]{1,0:T(8,128)}, /*index=5*/f32[144,512]{1,0:T(8,128)}) custom-call(s32[1]{0:T(128)S(6)} %copy.16.index_ref, bf16[256,512]{1,0:T(8,128)(2,1)} %get-tuple-element.15.key_in, f32[144,512]{1,0:T(8,128)} %get-tuple-element.16.grad_in, ...), custom_call_target="tpu_custom_call" | custom-call | tf_op jit(solution)/shard_map/pallas_call | solution.py:572

commit v3 on v2

--- a/solution.py
+++ b/solution.py
@@ -19,12 +19,12 @@
 
 
 def kernel(
-    tokens_hbm, gain_hbm, master_hbm, cot_hbm, global_hbm, local_hbm, index_ref,
-    key_ref, grad_ref, pseudo_ref,
-    tok, gain, master, frag_now, frag_local, cot, cot_oth,
+    tokens_hbm, gain_hbm, master_hbm, cot_hbm, global_hbm, local_hbm, moment_hbm, second_hbm, momentum_hbm, index_ref,
+    key_ref, master_ref, moment_ref, second_ref, global_ref, outer_ref,
+    tok, gain, master, old_moment, old_second, momentum, key_v, master_v, moment_v, second_v, global_v, outer_v, frag_now, frag_local, cot, cot_oth,
     w_own, w, norm, norm_oth, part, part_bf, e_in, s_in, s_sum, s_bf, e2_in, s2_in,
-    t_sum, t_bf, z_in, key_own, key_oth, key_in, diffs, r_in, r_sum,
-    in_sem, send_sem, recv_sem,
+    t_sum, t_bf, z_in, key_own, key_oth, key_in, diffs, re_in, rs_in, r_sum,
+    in_sem, out_sem, here_sem, send_sem, recv_sem,
 ):
     rows, cols = master.shape
     n_tok = tok.shape[0]
@@ -99,18 +99,40 @@
     load_cot = load(cot_hbm, cot)
     load_now = load(global_hbm, frag_now)
     load_loc = load(local_hbm, frag_local)
+    load_rest = [load(moment_hbm, old_moment), load(second_hbm, old_second), load(momentum_hbm, momentum)]
+    stores = []
+
+    def store(src, dst):
+        copy = pltpu.make_async_copy(src, dst, out_sem.at[len(stores)])
+        copy.start()
+        stores.append(copy)
+
 
     barrier = pltpu.get_barrier_semaphore()
     other_core = dev(y, z, x, 1 - core)
     peers = [along("x", 1), along("x", -1), along("y", 1), along("y", -1), other_core,
              dev(y, 1 - z, x, core), dev(y, 1 - z, x, 1 - core)]
-    peers += [{"rep": (rep + k) % REPS} for k in range(1, REPS)]
     for peer in peers:
         pl.semaphore_signal(barrier, inc=1, device_id=peer, device_id_type=MESH)
 
+    def rep_at(step):
+        return {"rep": (rep + step + REPS) % REPS}
+
+    STEP = (1, -1)
+    for step in STEP:
+        @pl.when(rep < (rep + step + REPS) % REPS)
+        def _():
+            pl.semaphore_signal(barrier, inc=1, device_id=rep_at(step), device_id_type=MESH)
+
+    lower = (rep + 1) // 2
+
     load_master.wait()
     w_own[...] = master[...].astype(BF16)
-    pl.semaphore_wait(barrier, len(peers))
+    pl.semaphore_wait(barrier, len(peers) + lower)
+    for step in STEP:
+        @pl.when(rep > (rep + step + REPS) % REPS)
+        def _():
+            pl.semaphore_signal(here_sem, inc=1, device_id=rep_at(step), device_id_type=MESH)
 
     def w_rows(y_, x_, c_):
         return y_, pl.ds(pl.multiple_of(x_ * pair + c_ * rows, 16), rows)
@@ -127,9 +149,6 @@
     @pl.when(jnp.logical_not(home))
     def _():
         push(w_own, own_at, other_core, w_near, w_got[0] + core)
-
-    load_cot.wait()
-    cot_copy = send(cot, cot_oth, other_core)
 
     tiles = group // 128
     n_group = norm.shape[0] * norm.shape[1]
@@ -157,12 +176,6 @@
         at = pl.ds(i * chunk, chunk)
         return send(norm.at[:, 1 - core, at], norm_oth.at[:, at], other_core)
 
-    load_gain.wait()
-    norm_copies = []
-    for i in range(n_chunk - 1):
-        normalise(i)
-        norm_copies.append(swap(i))
-
     first, second = ("x", "y"), ("y", "x")
     at1, at2 = (x, y), (y, x)
 
@@ -173,15 +186,7 @@
     def cut(where, columns):
         return (*where, columns)
 
-    STEP = (1, -1)
     SIDE_COLS = (lo, hi)
-    for c_ in range(2):
-        @pl.when(jnp.logical_not(jnp.logical_and(home, core == c_)))
-        def _():
-            pltpu.make_async_remote_copy(
-                src_ref=w_own, dst_ref=own_at, send_sem=send_sem.at[w_far], recv_sem=recv_sem.at[w_got[c_]],
-                device_id=other_core, device_id_type=MESH).wait_recv()
-
     rel = (0, -1, 1, 2)
     FULL = (pl.ds(0, cols), lo)
     SIDES = ((lo, hi), (pl.ds(0, half // 2), pl.ds(half // 2, half // 2)))
@@ -276,22 +281,110 @@
                     if i or j:
                         getattr(gz(hf, i, j), done)()
 
-    each_role(gather_start)
-
-    normalise(n_chunk - 1)
-    norm_copies.append(swap(n_chunk - 1))
+    def w_wait(c_):
+        pltpu.make_async_remote_copy(
+            src_ref=w_own, dst_ref=own_at, send_sem=send_sem.at[w_far], recv_sem=recv_sem.at[w_got[c_]],
+            device_id=other_core, device_id_type=MESH).wait_recv()
+
+    @pl.when(home)
+    def _():
+        for c_ in range(2):
+            @pl.when(core != c_)
+            def _():
+                w_wait(c_)
+        gather_start(0)
+
+    load_cot.wait()
+    cot_copy = send(cot, cot_oth, other_core)
+
+    load_gain.wait()
+    norm_copies = []
+    for i in range(2):
+        normalise(i)
+        norm_copies.append(swap(i))
+
+    @pl.when(jnp.logical_not(home))
+    def _():
+        for c_ in range(2):
+            w_wait(c_)
+        gather_start(1)
+
+    for i in range(2, n_chunk):
+        normalise(i)
+        norm_copies.append(swap(i))
 
     load_now.wait()
     load_loc.wait()
+    for copy in load_rest:
+        copy.wait()
     k = index_ref[0] % frag_now.shape[0]
-    diffs[...] = (frag_now[k] - frag_local[k]).astype(BF16)
+    diffs[...] = frag_now[k] - frag_local[k]
     quarter = cols // REPS
-
-    def quarter_of(r):
-        return diffs.at[:, pl.ds(pl.multiple_of(r * quarter, quarter), quarter)]
-
-    r_in[rep] = diffs[:, pl.ds(pl.multiple_of(rep * quarter, quarter), quarter)]
-    rep_copies = [send(quarter_of((rep + j) % REPS), r_in.at[rep], {"rep": (rep + j) % REPS}) for j in range(1, REPS)]
+    ROWS = (pl.ds(0, rows // 2), pl.ds(rows // 2, rows // 2))
+
+    def quarter_of(step, where):
+        r = (rep + step + REPS) % REPS
+        return where, pl.ds(pl.multiple_of(r * quarter, quarter), quarter)
+
+    def r_e(d):
+        return remote((6, d), diffs.at[quarter_of(2, ROWS[d])], re_in.at[d], rep_at(STEP[d]))
+
+    def r_d(d):
+        return remote((7, d), diffs.at[quarter_of(STEP[d], ROWS[1 - d])], rs_in.at[d, ROWS[1 - d]], rep_at(STEP[d]))
+
+    def r_c(d):
+        return remote((8, d), diffs.at[quarter_of(STEP[d], ROWS[d])], rs_in.at[d, ROWS[d]], rep_at(STEP[d]))
+
+    def r_g(d):
+        return remote((9, d), r_sum.at[rep], r_sum.at[rep], rep_at(STEP[d]))
+
+    def r_f(d):
+        ref = r_sum.at[(rep - STEP[d] + REPS) % REPS, ROWS[d]]
+        return remote((10, d), ref, ref, rep_at(STEP[d]))
+
+    def rep_start():
+        @pl.when(lower < 2)
+        def _():
+            pl.semaphore_wait(here_sem, 2 - lower)
+
+        for d in range(2):
+            r_e(d).start()
+        for d in range(2):
+            r_d(d).start()
+
+    def rep_combine():
+        for d in range(2):
+            r_e(d).wait_recv()
+            where = quarter_of(STEP[d], ROWS[d])
+            diffs[where] = diffs[where] + re_in[d]
+            r_c(d).start()
+
+    def rep_sum():
+        for d in range(2):
+            r_d(d).wait_recv()
+            r_c(d).wait_recv()
+        r_sum[rep] = diffs[quarter_of(0, pl.ds(0, rows))] + rs_in[0] + rs_in[1]
+        for d in range(2):
+            r_g(d).start()
+
+    def rep_forward():
+        for d in range(2):
+            r_g(d).wait_recv()
+            r_f(d).start()
+
+    def rep_end():
+        for d in range(2):
+            r_f(d).wait_recv()
+        round_count = (index_ref[0] // NFRAG).astype(F32)
+        outer_rate = 0.7 * (1.0 - round_count / 512.0)
+        for r in range(REPS):
+            at = pl.ds(r * quarter, quarter)
+            pseudo = r_sum[r] / REPS
+            outer = 0.9 * momentum[k, :, at] + pseudo
+            outer_v[:, at] = outer
+            global_v[:, at] = frag_now[k, :, at] - outer_rate * (pseudo + 0.9 * outer)
+        store(outer_v, outer_ref)
+        store(global_v, global_ref)
 
     piece = group // 3
     over_tokens = (((0,), (0,)), ((), ()))
@@ -303,7 +396,6 @@
                 norm[q, core, :, j * piece:(j + 1) * piece], cot[...], over_tokens, preferred_element_type=F32)
 
     each_role(gather_first)
-
     cot_copy.wait_recv()
     for copy in norm_copies:
         copy.wait_recv()
@@ -320,14 +412,14 @@
     e_copies = [[None] * SIDE, [None] * SIDE]
     d_copies = [[None] * SIDE, [None] * SIDE]
     c_copies = [[None] * SIDE, [None] * SIDE]
-    for i in order:
+    def spread(i):
         for hf in range(2):
             a = at1[hf] + rel[i] + SIDE
             e_copies[hf][i] = [
                 send(part_bf.at[cut(block(hf, a, at2[hf] + 2), SIDE_COLS[d])], e_in.at[hf, d, i], along(second[hf], STEP[d]))
                 for d in range(2)]
-    each_role(gather_turn)
-    for i in order:
+
+    def direct(i):
         for hf in range(2):
             a = at1[hf] + rel[i] + SIDE
             d_copies[hf][i] = [
@@ -367,43 +459,51 @@
                 d2_copies[hf][d] = send(
                     s_bf.at[hf, i, :, SIDE_COLS[1 - d]], s2_in.at[hf, d, :, SIDE_COLS[1 - d]], along(first[hf], STEP[d]))
 
+    c2_copies = [[None, None], [None, None]]
+
+    def cross():
+        for hf in range(2):
+            for d in range(2):
+                i = 2 - d
+                e2_copies[hf][d].wait_recv()
+                s_bf[hf, i, :, SIDE_COLS[d]] = (s_sum[hf, i, :, SIDE_COLS[d]] + e2_in[hf, d].astype(F32)).astype(BF16)
+                c2_copies[hf][d] = send(
+                    s_bf.at[hf, i, :, SIDE_COLS[d]], s2_in.at[hf, d, :, SIDE_COLS[d]], along(first[hf], STEP[d]))
+
     def on(i):
         each_role(lambda role: [gather_on(role, hf, i) for hf in range(2)])
 
     def last(i):
         each_role(lambda role: gather_last(role, i))
 
+    spread(3)
+    spread(2)
+    spread(1)
+    spread(0)
+    each_role(gather_turn)
+    rep_start()
     combine(3)
+    direct(3)
     combine(2)
+    direct(2)
     on(1)
     on(2)
-
-    for copy in rep_copies:
-        copy.wait_recv()
-    r_sum[rep] = (r_in[0].astype(F32) + r_in[1].astype(F32) + r_in[2].astype(F32) + r_in[3].astype(F32)).astype(BF16)
-    sum_copies = [send(r_sum.at[rep], r_sum.at[rep], {"rep": (rep + j) % REPS}) for j in range(1, REPS)]
-
+    rep_combine()
     combine(1)
+    direct(1)
     settle(3)
     on(3)
     last(0)
     combine(0)
+    direct(0)
+    rep_sum()
     last(1)
     last(2)
     settle(2)
     settle(1)
-
-    c2_copies = [[None, None], [None, None]]
-    for hf in range(2):
-        for d in range(2):
-            i = 2 - d
-            e2_copies[hf][d].wait_recv()
-            s_bf[hf, i, :, SIDE_COLS[d]] = (s_sum[hf, i, :, SIDE_COLS[d]] + e2_in[hf, d].astype(F32)).astype(BF16)
-            c2_copies[hf][d] = send(
-                s_bf.at[hf, i, :, SIDE_COLS[d]], s2_in.at[hf, d, :, SIDE_COLS[d]], along(first[hf], STEP[d]))
-
+    rep_forward()
+    cross()
     last(3)
-
     settle(0)
     for hf in range(2):
         for d in range(2):
@@ -425,26 +525,37 @@
         push(t_bf.at[0], z_in.at[1], dev(y, core, x, 0), z_far0, z_got[1])
         push(t_bf.at[1], z_in.at[1], dev(y, core, x, 1), z_far1, z_got[1])
 
-    @pl.when(jnp.logical_not(home))
-    def _():
-        gather_far("wait_recv")
-
-    def keys(operand):
-        total = jnp.dot(operand(0), w[0], preferred_element_type=F32)
-        for q in range(1, SIDE):
-            total = total + jnp.dot(operand(q), w[q], preferred_element_type=F32)
+    def in_last(hf, i, j):
+        return (j if hf == 0 else i) == 3
+
+    def far_wait(late):
+        @pl.when(jnp.logical_not(home))
+        def _():
+            for hf in range(2):
+                for i in range(SIDE):
+                    for j in range(SIDE):
+                        if (i or j) and in_last(hf, i, j) == late:
+                            gz(hf, i, j).wait_recv()
+
+    def key_terms(operand, steps):
+        total = None
+        for step in steps:
+            q = (y + step) % SIDE
+            term = jnp.dot(operand(q), w[q], preferred_element_type=F32)
+            total = term if total is None else total + term
         return total
 
-    key_oth[...] = keys(lambda q: norm_oth[q])
+    far_wait(False)
+    key_oth[...] = key_terms(lambda q: norm_oth[q], (0, 1, 3))
+    key_own[...] = key_terms(lambda q: norm[q, core], (0, 1, 3))
+    far_wait(True)
+    key_oth[...] = key_oth[...] + key_terms(lambda q: norm_oth[q], (2,))
     key_copy = send(key_oth, key_in, other_core)
-    key_own[...] = keys(lambda q: norm[q, core])
+    key_own[...] = key_own[...] + key_terms(lambda q: norm[q, core], (2,))
+    rep_end()
     key_copy.wait_recv()
-    key_ref[...] = (key_own[...] + key_in[...]).astype(BF16)
-
-    for copy in sum_copies:
-        copy.wait_recv()
-    for r in range(REPS):
-        pseudo_ref[:, r * quarter:(r + 1) * quarter] = r_sum[r].astype(F32) / REPS
+    key_v[...] = (key_own[...] + key_in[...]).astype(BF16)
+    store(key_v, key_ref)
 
     def z_copy(sem, got):
         return pltpu.make_async_remote_copy(
@@ -453,14 +564,27 @@
 
     z_copy(z_far0, z_got[1]).wait_recv()
 
+    def step_with(near):
+        grad = near + z_in[1].astype(F32)
+        old = master[...]
+        moment_next = 0.9 * old_moment[...] + 0.1 * grad
+        second_next = 0.95 * old_second[...] + 0.05 * grad * grad
+        moment_v[...] = moment_next
+        second_v[...] = second_next
+        master_v[...] = old - 0.02 * (moment_next / (jnp.sqrt(second_next) + 1e-08) + 0.1 * old)
+
     @pl.when(home)
     def _():
-        grad_ref[...] = t_sum[core] + z_in[1].astype(F32)
+        step_with(t_sum[core])
 
     @pl.when(jnp.logical_not(home))
     def _():
         z_copy(z_near, z_got[0]).wait_recv()
-        grad_ref[...] = z_in[0].astype(F32) + z_in[1].astype(F32)
+        step_with(z_in[0].astype(F32))
+
+    store(master_v, master_ref)
+    store(moment_v, moment_ref)
+    store(second_v, second_ref)
 
     far_copy.wait_send()
 
@@ -480,31 +604,38 @@
     def _():
         gather_far("wait_send")
 
+    for d in range(2):
+        for copy in (r_e(d), r_d(d), r_c(d), r_g(d), r_f(d)):
+            copy.wait_send()
+
     for copy in started:
         copy.wait_send()
-
-
-def exchange(tokens, gain, master, cot, frag_global, frag_local, index):
+    for copy in stores:
+        copy.wait()
+
+
+def exchange(tokens, gain, master, cot, frag_global, frag_local, moment, second, momentum, index):
     n_tok, width = tokens.shape
     rows, cols = master.shape
     n_group = SIDE * PLANES
     group = width // n_group
     half = cols // 2
     any_spec = pl.BlockSpec(memory_space=pl.ANY)
-    vmem_spec = pl.BlockSpec(memory_space=pltpu.VMEM)
+    rows_f32 = jax.ShapeDtypeStruct((rows, cols), F32)
     return pl.pallas_call(
         kernel,
-        out_shape=(
-            jax.ShapeDtypeStruct((n_tok, cols), BF16),
-            jax.ShapeDtypeStruct((rows, cols), F32),
-            jax.ShapeDtypeStruct((rows, cols), F32),
-        ),
-        in_specs=[any_spec] * 6 + [pl.BlockSpec(memory_space=pltpu.SMEM)],
-        out_specs=(vmem_spec,) * 3,
+        out_shape=(jax.ShapeDtypeStruct((n_tok, cols), BF16),) + (rows_f32,) * 5,
+        in_specs=[any_spec] * 9 + [pl.BlockSpec(memory_space=pltpu.SMEM)],
+        out_specs=(any_spec,) * 6,
         scratch_shapes=[
             pltpu.VMEM((n_tok, width), BF16),
             pltpu.VMEM((1, width), F32),
             pltpu.VMEM((rows, cols), F32),
+            pltpu.VMEM((rows, cols), F32),
+            pltpu.VMEM((rows, cols), F32),
+            pltpu.VMEM(momentum.shape, F32),
+            pltpu.VMEM((n_tok, cols), BF16),
+        ] + [pltpu.VMEM((rows, cols), F32)] * 5 + [
             pltpu.VMEM(frag_global.shape, F32),
             pltpu.VMEM(frag_local.shape, F32),
             pltpu.VMEM((n_tok, cols), BF16),
@@ -527,10 +658,13 @@
             pltpu.VMEM((n_tok, cols), F32),
             pltpu.VMEM((n_tok, cols), F32),
             pltpu.VMEM((n_tok, cols), F32),
-            pltpu.VMEM((rows, cols), BF16),
-            pltpu.VMEM((REPS, rows, cols // REPS), BF16),
-            pltpu.VMEM((REPS, rows, cols // REPS), BF16),
-            pltpu.SemaphoreType.DMA((12,)),
+            pltpu.VMEM((rows, cols), F32),
+            pltpu.VMEM((2, rows // 2, cols // REPS), F32),
+            pltpu.VMEM((2, rows, cols // REPS), F32),
+            pltpu.VMEM((REPS, rows, cols // REPS), F32),
+            pltpu.SemaphoreType.DMA((16,)),
+            pltpu.SemaphoreType.DMA((6,)),
+            pltpu.SemaphoreType.REGULAR,
             pltpu.SemaphoreType.DMA((N_SEMS,)),
             pltpu.SemaphoreType.DMA((N_SEMS,)),
         ],
@@ -538,47 +672,34 @@
             collective_id=0, has_side_effects=True, vmem_limit_bytes=60 * 1024 * 1024
         ),
         cost_estimate=pl.CostEstimate(flops=4 * n_tok * width * cols, bytes_accessed=10 * 1024 * 1024, transcendentals=0),
-    )(tokens, gain, master, cot, frag_global, frag_local, index)
-
-
-def update_kernel(
-    index_ref, key_in, grad_in, pseudo_in, master, moment, second, frag_now, momentum,
-    key_out, master_out, moment_out, second_out, global_out, outer_out,
-):
-    key_out[...] = key_in[...]
-    grad = grad_in[...]
-    moment_next = 0.9 * moment[...] + 0.1 * grad
-    second_next = 0.95 * second[...] + 0.05 * grad * grad
-    old = master[...]
-    moment_out[...] = moment_next
-    second_out[...] = second_next
-    master_out[...] = old - 0.02 * (moment_next / (jnp.sqrt(second_next) + 1e-08) + 0.1 * old)
-    round_count = (index_ref[0] // NFRAG).astype(F32)
-    outer_rate = 0.7 * (1.0 - round_count / 512.0)
-    pseudo = pseudo_in[...]
-    new_outer = 0.9 * momentum[...] + pseudo
-    outer_out[...] = new_outer
-    global_out[...] = frag_now[...] - outer_rate * (pseudo + 0.9 * new_outer)
-
-
-def update(index, key_rows, grad, pseudo, master, moment, second, frag_global, momentum):
-    steps = 2
-    rows, cols = grad.shape
-    n_tok = key_rows.shape[0]
-    key_spec = pl.BlockSpec((n_tok // steps, cols), lambda i, index: (i, 0))
-    row_spec = pl.BlockSpec((rows // steps, cols), lambda i, index: (i, 0))
-    frag_spec = pl.BlockSpec((None, rows // steps, cols), lambda i, index: (index[0] % NFRAG, i, 0))
-    rows_f32 = jax.ShapeDtypeStruct((rows, cols), F32)
+    )(tokens, gain, master, cot, frag_global, frag_local, moment, second, momentum, index)
+
+
+def pass_kernel(*refs):
+    n = (len(refs) - 2) // 3
+    in_sem, out_sem = refs[-2:]
+    reads = [pltpu.make_async_copy(refs[i], refs[2 * n + i], in_sem.at[i]) for i in range(n)]
+    writes = [pltpu.make_async_copy(refs[2 * n + i], refs[n + i], out_sem.at[i]) for i in range(n)]
+    for copy in reads:
+        copy.start()
+    for i in range(n):
+        reads[i].wait()
+        writes[i].start()
+    for copy in writes:
+        copy.wait()
+
+
+def pass_on(arrays):
+    any_spec = pl.BlockSpec(memory_space=pl.ANY)
+    n = len(arrays)
     return pl.pallas_call(
-        update_kernel,
-        out_shape=(jax.ShapeDtypeStruct(key_rows.shape, BF16),) + (rows_f32,) * 5,
-        grid_spec=pltpu.PrefetchScalarGridSpec(
-            num_scalar_prefetch=1,
-            grid=(steps,),
-            in_specs=[key_spec] + [row_spec] * 5 + [frag_spec] * 2,
-            out_specs=(key_spec,) + (row_spec,) * 5,
-        ),
-    )(index, key_rows, grad, pseudo, master, moment, second, frag_global, momentum)
+        pass_kernel,
+        out_shape=tuple(jax.ShapeDtypeStruct(a.shape, a.dtype) for a in arrays),
+        in_specs=[any_spec] * n,
+        out_specs=(any_spec,) * n,
+        scratch_shapes=[pltpu.VMEM(a.shape, a.dtype) for a in arrays]
+        + [pltpu.SemaphoreType.DMA((n,)), pltpu.SemaphoreType.DMA((n,))],
+    )(*arrays)
 
 
 def shards(
@@ -593,11 +714,9 @@
     outer_momentum,
     fragment_index,
 ):
-    master = master_weight[0]
-    key_rows, grad, pseudo_grad = exchange(
-        tokens[0], norm_gain[None], master, cotangent[0], frag_global, frag_local[0], fragment_index)
-    key_rows, master_next, moment_next, second_next, new_global, new_outer = update(
-        fragment_index, key_rows, grad, pseudo_grad, master, inner_moment[0], inner_second[0], frag_global, outer_momentum)
+    key_rows, master_next, moment_next, second_next, new_global, new_outer = pass_on(exchange(
+        tokens[0], norm_gain[None], master_weight[0], cotangent[0], frag_global, frag_local[0],
+        inner_moment[0], inner_second[0], outer_momentum, fragment_index))
     return (
         key_rows[None],
         master_next[None],

time: 71.5 us -> 66.3 us (0.927)
  Pallas kernels: 69.4 us -> 64.8 us
    pallas_call x1, Pallas kernels: 66.7 us -> 62.6 us  [exchange(): pl.pallas_call(kernel, out_shape=(jax.ShapeDtypeStruct((n_tok, cols), BF1...]
where the time goes in v3:
time: 66.3 us; the launch traced here: 66.1 us
  Pallas kernels  64.8 us (98%)
  between operations  1.29 us (2%)
    pallas_call x1, Pallas kernels, exchange(): pl.pallas_call(kernel, out_shape=(jax.ShapeDtypeStruct((n_tok, cols), BF1...  62.6 us
    pallas_call x1, Pallas kernels, pass_on(): pl.pallas_call(pass_kernel, out_shape=tuple((jax.ShapeDtypeStruct(a.shape...  2.25 us

profile of v3, /device:TPU:1, one launch (start us, length us, event | category | flops | bytes accessed | tf_op | source)
XLA Modules:
  0.0 66.1 jit_solution(8422376941811648465)
XLA Ops:
  1.3 62.6 %shard_map.145 = (bf16[256,512]{1,0:T(8,128)(2,1)}, f32[144,512]{1,0:T(8,128)}, f32[144,512]{1,0:T(8,128)}, f32[144,512]{1,0:T(8,128)}, f32[144,512]{1,0:T(8,128)}, /*index=5*/f32[144,512]{1,0:T(8,128)}) custom-call(bf16[256,9216]{1,0:T(8,128)(2,1)} %bitcast.11, f32[1,9216]{1,0:T(1,128)} %bitcast.21, f32[144,512]{1,0:T(8,128)} %bitcast.13, ...), custom_call_target="tpu_custom_call" | custom-call | flops 4831838208 | bytes 10485760 | tf_op jit(solution)/shard_map/pallas_call | solution.py:625
  63.9 2.2 %shard_map.146 = (bf16[256,512]{1,0:T(8,128)(2,1)}, f32[144,512]{1,0:T(8,128)}, f32[144,512]{1,0:T(8,128)}, f32[144,512]{1,0:T(8,128)}, f32[144,512]{1,0:T(8,128)}, /*index=5*/f32[144,512]{1,0:T(8,128)}) custom-call(bf16[256,512]{1,0:T(8,128)(2,1)} %get-tuple-element.18.refs_0_, f32[144,512]{1,0:T(8,128)} %get-tuple-element.19.refs_1_, ...), custom_call_target="tpu_custom_call" | custom-call | tf_op jit(solution)/shard_map/pallas_call | solution.py:695

commit v4 on v3

--- a/solution.py
+++ b/solution.py
@@ -317,8 +317,13 @@
     load_loc.wait()
     for copy in load_rest:
         copy.wait()
-    k = index_ref[0] % frag_now.shape[0]
-    diffs[...] = frag_now[k] - frag_local[k]
+    odd = index_ref[...] % NFRAG == 1
+
+    def picked(ref, *where):
+        return jnp.where(odd, ref[(1, *where)], ref[(0, *where)])
+
+    everything = pl.ds(0, rows), pl.ds(0, cols)
+    diffs[...] = picked(frag_now, *everything) - picked(frag_local, *everything)
     quarter = cols // REPS
     ROWS = (pl.ds(0, rows // 2), pl.ds(rows // 2, rows // 2))
 
@@ -375,14 +380,14 @@
     def rep_end():
         for d in range(2):
             r_f(d).wait_recv()
-        round_count = (index_ref[0] // NFRAG).astype(F32)
+        round_count = (index_ref[...] // NFRAG).astype(F32)
         outer_rate = 0.7 * (1.0 - round_count / 512.0)
         for r in range(REPS):
             at = pl.ds(r * quarter, quarter)
             pseudo = r_sum[r] / REPS
-            outer = 0.9 * momentum[k, :, at] + pseudo
+            outer = 0.9 * picked(momentum, pl.ds(0, rows), at) + pseudo
             outer_v[:, at] = outer
-            global_v[:, at] = frag_now[k, :, at] - outer_rate * (pseudo + 0.9 * outer)
+            global_v[:, at] = picked(frag_now, pl.ds(0, rows), at) - outer_rate * (pseudo + 0.9 * outer)
         store(outer_v, outer_ref)
         store(global_v, global_ref)
 
@@ -476,32 +481,32 @@
     def last(i):
         each_role(lambda role: gather_last(role, i))
 
+    rep_start()
     spread(3)
     spread(2)
     spread(1)
     spread(0)
     each_role(gather_turn)
-    rep_start()
+    rep_combine()
     combine(3)
     direct(3)
     combine(2)
     direct(2)
     on(1)
+    combine(1)
     on(2)
-    rep_combine()
-    combine(1)
     direct(1)
+    rep_sum()
     settle(3)
     on(3)
+    combine(0)
     last(0)
-    combine(0)
     direct(0)
-    rep_sum()
+    rep_forward()
     last(1)
+    settle(2)
     last(2)
-    settle(2)
     settle(1)
-    rep_forward()
     cross()
     last(3)
     settle(0)
@@ -549,13 +554,19 @@
     key_oth[...] = key_terms(lambda q: norm_oth[q], (0, 1, 3))
     key_own[...] = key_terms(lambda q: norm[q, core], (0, 1, 3))
     far_wait(True)
-    key_oth[...] = key_oth[...] + key_terms(lambda q: norm_oth[q], (2,))
-    key_copy = send(key_oth, key_in, other_core)
+    key_copies = []
+    half_rows = n_tok // 2
+    for h in range(2):
+        at = pl.ds(h * half_rows, half_rows)
+        key_oth[at, :] = key_oth[at, :] + key_terms(lambda q: norm_oth[q, at], (2,))
+        key_copies.append(send(key_oth.at[at], key_in.at[at], other_core))
     key_own[...] = key_own[...] + key_terms(lambda q: norm[q, core], (2,))
     rep_end()
-    key_copy.wait_recv()
-    key_v[...] = (key_own[...] + key_in[...]).astype(BF16)
-    store(key_v, key_ref)
+    for h in range(2):
+        at = pl.ds(h * half_rows, half_rows)
+        key_copies[h].wait_recv()
+        key_v[at, :] = (key_own[at, :] + key_in[at, :]).astype(BF16)
+        store(key_v.at[at], key_ref.at[at])
 
     def z_copy(sem, got):
         return pltpu.make_async_remote_copy(
@@ -625,7 +636,7 @@
     return pl.pallas_call(
         kernel,
         out_shape=(jax.ShapeDtypeStruct((n_tok, cols), BF16),) + (rows_f32,) * 5,
-        in_specs=[any_spec] * 9 + [pl.BlockSpec(memory_space=pltpu.SMEM)],
+        in_specs=[any_spec] * 9 + [pl.BlockSpec(memory_space=pltpu.VMEM)],
         out_specs=(any_spec,) * 6,
         scratch_shapes=[
             pltpu.VMEM((n_tok, width), BF16),
@@ -663,7 +674,7 @@
             pltpu.VMEM((2, rows, cols // REPS), F32),
             pltpu.VMEM((REPS, rows, cols // REPS), F32),
             pltpu.SemaphoreType.DMA((16,)),
-            pltpu.SemaphoreType.DMA((6,)),
+            pltpu.SemaphoreType.DMA((8,)),
             pltpu.SemaphoreType.REGULAR,
             pltpu.SemaphoreType.DMA((N_SEMS,)),
             pltpu.SemaphoreType.DMA((N_SEMS,)),
@@ -716,7 +727,7 @@
 ):
     key_rows, master_next, moment_next, second_next, new_global, new_outer = pass_on(exchange(
         tokens[0], norm_gain[None], master_weight[0], cotangent[0], frag_global, frag_local[0],
-        inner_moment[0], inner_second[0], outer_momentum, fragment_index))
+        inner_moment[0], inner_second[0], outer_momentum, fragment_index[None]))
     return (
         key_rows[None],
         master_next[None],

time: 66.3 us -> 65.1 us (0.982)
  Pallas kernels: 64.8 us -> 63.7 us
    pallas_call x1, Pallas kernels: 62.6 us -> 61.4 us  [exchange(): pl.pallas_call(kernel, out_shape=(jax.ShapeDtypeStruct((n_tok, cols), BF1...]
where the time goes in v4:
time: 65.1 us; the launch traced here: 64.9 us
  Pallas kernels  63.7 us (98%)
  between operations  1.29 us (2%)
    pallas_call x1, Pallas kernels, exchange(): pl.pallas_call(kernel, out_shape=(jax.ShapeDtypeStruct((n_tok, cols), BF1...  61.4 us
    pallas_call x1, Pallas kernels, pass_on(): pl.pallas_call(pass_kernel, out_shape=tuple((jax.ShapeDtypeStruct(a.shape...  2.25 us

profile of v4, /device:TPU:1, one launch (start us, length us, event | category | flops | bytes accessed | tf_op | source)
XLA Modules:
  0.0 64.9 jit_solution(8324529509424177300)
XLA Ops:
  1.3 61.4 %shard_map.145 = (bf16[256,512]{1,0:T(8,128)(2,1)}, f32[144,512]{1,0:T(8,128)}, f32[144,512]{1,0:T(8,128)}, f32[144,512]{1,0:T(8,128)}, f32[144,512]{1,0:T(8,128)}, /*index=5*/f32[144,512]{1,0:T(8,128)}) custom-call(bf16[256,9216]{1,0:T(8,128)(2,1)} %bitcast.13, f32[1,9216]{1,0:T(1,128)} %bitcast.23, f32[144,512]{1,0:T(8,128)} %bitcast.15, ...), custom_call_target="tpu_custom_call" | custom-call | flops 4831838208 | bytes 10485760 | tf_op jit(solution)/shard_map/pallas_call | solution.py:636
  62.7 2.2 %shard_map.146 = (bf16[256,512]{1,0:T(8,128)(2,1)}, f32[144,512]{1,0:T(8,128)}, f32[144,512]{1,0:T(8,128)}, f32[144,512]{1,0:T(8,128)}, f32[144,512]{1,0:T(8,128)}, /*index=5*/f32[144,512]{1,0:T(8,128)}) custom-call(bf16[256,512]{1,0:T(8,128)(2,1)} %get-tuple-element.18.refs_0_, f32[144,512]{1,0:T(8,128)} %get-tuple-element.19.refs_1_, ...), custom_call_target="tpu_custom_call" | custom-call | tf_op jit(solution)/shard_map/pallas_call | solution.py:706

commit v5 on v4

--- a/solution.py
+++ b/solution.py
@@ -140,7 +140,11 @@
     own_at = w.at[w_rows(y, x, core)]
     w_far, w_near = slot(), slot()
     w_got = (slot(), slot())
-    far_copy = push(w_own, own_at, dev(y, 1 - z, x, z), w_far, w_got[0] + core)
+    w_far_hi = slot()
+    w_got_hi = (slot(), slot())
+    own_place = w_rows(y, x, core)
+    far_copy = push(w_own.at[:, lo], w.at[(*own_place, lo)], dev(y, 1 - z, x, z), w_far, w_got[0] + core)
+    far_copy_hi = push(w_own.at[:, hi], w.at[(*own_place, hi)], dev(y, 1 - z, x, z), w_far_hi, w_got_hi[0] + core)
 
     @pl.when(home)
     def _():
@@ -281,9 +285,9 @@
                     if i or j:
                         getattr(gz(hf, i, j), done)()
 
-    def w_wait(c_):
+    def w_wait(got, src, dst):
         pltpu.make_async_remote_copy(
-            src_ref=w_own, dst_ref=own_at, send_sem=send_sem.at[w_far], recv_sem=recv_sem.at[w_got[c_]],
+            src_ref=src, dst_ref=dst, send_sem=send_sem.at[w_far], recv_sem=recv_sem.at[got],
             device_id=other_core, device_id_type=MESH).wait_recv()
 
     @pl.when(home)
@@ -291,7 +295,7 @@
         for c_ in range(2):
             @pl.when(core != c_)
             def _():
-                w_wait(c_)
+                w_wait(w_got[c_], w_own, own_at)
         gather_start(0)
 
     load_cot.wait()
@@ -306,7 +310,7 @@
     @pl.when(jnp.logical_not(home))
     def _():
         for c_ in range(2):
-            w_wait(c_)
+            w_wait(w_got[c_], w_own.at[:, lo], w.at[(*own_place, lo)])
         gather_start(1)
 
     for i in range(2, n_chunk):
@@ -550,6 +554,11 @@
             total = term if total is None else total + term
         return total
 
+    @pl.when(jnp.logical_not(home))
+    def _():
+        for c_ in range(2):
+            w_wait(w_got_hi[c_], w_own.at[:, hi], w.at[(*own_place, hi)])
+
     far_wait(False)
     key_oth[...] = key_terms(lambda q: norm_oth[q], (0, 1, 3))
     key_own[...] = key_terms(lambda q: norm[q, core], (0, 1, 3))
@@ -598,6 +607,7 @@
     store(second_v, second_ref)
 
     far_copy.wait_send()
+    far_copy_hi.wait_send()
 
     @pl.when(home)
     def _():

time: 65.1 us -> 64.2 us (0.986)
  Pallas kernels: 63.7 us -> 62.8 us
    pallas_call x1, Pallas kernels: 61.4 us -> 60.6 us  [exchange(): pl.pallas_call(kernel, out_shape=(jax.ShapeDtypeStruct((n_tok, cols), BF1...]
where the time goes in v5:
time: 64.2 us; the launch traced here: 64.1 us
  Pallas kernels  62.8 us (98%)
  between operations  1.29 us (2%)
    pallas_call x1, Pallas kernels, exchange(): pl.pallas_call(kernel, out_shape=(jax.ShapeDtypeStruct((n_tok, cols), BF1...  60.6 us
    pallas_call x1, Pallas kernels, pass_on(): pl.pallas_call(pass_kernel, out_shape=tuple((jax.ShapeDtypeStruct(a.shape...  2.25 us

profile of v5, /device:TPU:1, one launch (start us, length us, event | category | flops | bytes accessed | tf_op | source)
XLA Modules:
  0.0 64.1 jit_solution(15521779280856923109)
XLA Ops:
  1.3 60.6 %shard_map.145 = (bf16[256,512]{1,0:T(8,128)(2,1)}, f32[144,512]{1,0:T(8,128)}, f32[144,512]{1,0:T(8,128)}, f32[144,512]{1,0:T(8,128)}, f32[144,512]{1,0:T(8,128)}, /*index=5*/f32[144,512]{1,0:T(8,128)}) custom-call(bf16[256,9216]{1,0:T(8,128)(2,1)} %bitcast.13, f32[1,9216]{1,0:T(1,128)} %bitcast.23, f32[144,512]{1,0:T(8,128)} %bitcast.15, ...), custom_call_target="tpu_custom_call" | custom-call | flops 4831838208 | bytes 10485760 | tf_op jit(solution)/shard_map/pallas_call | solution.py:646
  61.9 2.2 %shard_map.146 = (bf16[256,512]{1,0:T(8,128)(2,1)}, f32[144,512]{1,0:T(8,128)}, f32[144,512]{1,0:T(8,128)}, f32[144,512]{1,0:T(8,128)}, f32[144,512]{1,0:T(8,128)}, /*index=5*/f32[144,512]{1,0:T(8,128)}) custom-call(bf16[256,512]{1,0:T(8,128)(2,1)} %get-tuple-element.18.refs_0_, f32[144,512]{1,0:T(8,128)} %get-tuple-element.19.refs_1_, ...), custom_call_target="tpu_custom_call" | custom-call | tf_op jit(solution)/shard_map/pallas_call | solution.py:716

commit v6 on v5

--- a/solution.py
+++ b/solution.py
@@ -140,19 +140,19 @@
     own_at = w.at[w_rows(y, x, core)]
     w_far, w_near = slot(), slot()
     w_got = (slot(), slot())
+    @pl.when(home)
+    def _():
+        w[w_rows(y, x, core)] = w_own[...]
+
+    @pl.when(jnp.logical_not(home))
+    def _():
+        push(w_own, own_at, other_core, w_near, w_got[0] + core)
+
     w_far_hi = slot()
     w_got_hi = (slot(), slot())
     own_place = w_rows(y, x, core)
     far_copy = push(w_own.at[:, lo], w.at[(*own_place, lo)], dev(y, 1 - z, x, z), w_far, w_got[0] + core)
     far_copy_hi = push(w_own.at[:, hi], w.at[(*own_place, hi)], dev(y, 1 - z, x, z), w_far_hi, w_got_hi[0] + core)
-
-    @pl.when(home)
-    def _():
-        w[w_rows(y, x, core)] = w_own[...]
-
-    @pl.when(jnp.logical_not(home))
-    def _():
-        push(w_own, own_at, other_core, w_near, w_got[0] + core)
 
     tiles = group // 128
     n_group = norm.shape[0] * norm.shape[1]
@@ -227,13 +227,11 @@
         def _():
             step(1)
 
-    def gather_start(role):
-        for hf in range(2):
-            for d in range(2):
-                g1(role, hf, d).start()
-        for hf in range(2):
-            for d in range(2):
-                g2(role, hf, 0, d).start()
+    def gather_start(role, hf):
+        for d in range(2):
+            g1(role, hf, d).start()
+        for d in range(2):
+            g2(role, hf, 0, d).start()
 
     def gather_first(role):
         for hf in range(2):
@@ -293,10 +291,15 @@
     @pl.when(home)
     def _():
         for c_ in range(2):
+            @pl.when(core == c_)
+            def _():
+                gather_start(0, c_)
+
+        for c_ in range(2):
             @pl.when(core != c_)
             def _():
                 w_wait(w_got[c_], w_own, own_at)
-        gather_start(0)
+                gather_start(0, c_)
 
     load_cot.wait()
     cot_copy = send(cot, cot_oth, other_core)
@@ -311,7 +314,7 @@
     def _():
         for c_ in range(2):
             w_wait(w_got[c_], w_own.at[:, lo], w.at[(*own_place, lo)])
-        gather_start(1)
+            gather_start(1, c_)
 
     for i in range(2, n_chunk):
         normalise(i)

time: 64.2 us -> 64.1 us (level)
  no operation moved by 1% of the time
where the time goes in v6:
time: 64.1 us; the launch traced here: 64 us
  Pallas kernels  62.7 us (98%)
  between operations  1.29 us (2%)
    pallas_call x1, Pallas kernels, exchange(): pl.pallas_call(kernel, out_shape=(jax.ShapeDtypeStruct((n_tok, cols), BF1...  60.5 us
    pallas_call x1, Pallas kernels, pass_on(): pl.pallas_call(pass_kernel, out_shape=tuple((jax.ShapeDtypeStruct(a.shape...  2.25 us

profile of v6, /device:TPU:1, one launch (start us, length us, event | category | flops | bytes accessed | tf_op | source)
XLA Modules:
  0.0 64.0 jit_solution(6811968761428002491)
XLA Ops:
  1.3 60.5 %shard_map.145 = (bf16[256,512]{1,0:T(8,128)(2,1)}, f32[144,512]{1,0:T(8,128)}, f32[144,512]{1,0:T(8,128)}, f32[144,512]{1,0:T(8,128)}, f32[144,512]{1,0:T(8,128)}, /*index=5*/f32[144,512]{1,0:T(8,128)}) custom-call(bf16[256,9216]{1,0:T(8,128)(2,1)} %bitcast.13, f32[1,9216]{1,0:T(1,128)} %bitcast.23, f32[144,512]{1,0:T(8,128)} %bitcast.15, ...), custom_call_target="tpu_custom_call" | custom-call | flops 4831838208 | bytes 10485760 | tf_op jit(solution)/shard_map/pallas_call | solution.py:649
  61.8 2.2 %shard_map.146 = (bf16[256,512]{1,0:T(8,128)(2,1)}, f32[144,512]{1,0:T(8,128)}, f32[144,512]{1,0:T(8,128)}, f32[144,512]{1,0:T(8,128)}, f32[144,512]{1,0:T(8,128)}, /*index=5*/f32[144,512]{1,0:T(8,128)}) custom-call(bf16[256,512]{1,0:T(8,128)(2,1)} %get-tuple-element.18.refs_0_, f32[144,512]{1,0:T(8,128)} %get-tuple-element.19.refs_1_, ...), custom_call_target="tpu_custom_call" | custom-call | tf_op jit(solution)/shard_map/pallas_call | solution.py:719
